TPU v7x, 256 devices: a whole 4x4x8 slice. The times are simulated.
256 devices in a mesh: dp: 32 (over z_lo, y, core), mp: 8 (over x, z_hi).
Axes of the slice: x: 4, y: 4, z: 8 (z_hi: 2, z_lo: 4; z = z_hi * 4 + z_lo), core: 2. Of those that a mesh axis runs over, the one named last changes fastest.
Arguments:
- gradient: bfloat16 [32, 2, 96, 28672], P('dp', None, None, 'mp'), may hold values from -180 to 180
- feedback: float32 [32, 2, 96, 28672], P('dp', None, None, 'mp'), may hold values from -6 to 6
- right_initial: float32 [2, 28672, 32], P(None, 'mp'), may hold values from -6 to 6
Outputs:
- decoded: float32 [2, 96, 28672], P(None, None, 'mp')
- carried: float32 [32, 2, 96, 28672], P('dp', None, None, 'mp')
All inputs are finite; a program needn't handle non-finite values.
Results may differ from a plain program's by a relative error of at most 0.0003.
Values sent between devices are 32-bit elements; how exact they have to be, the bound alone decides.
A program may use at most 64 MiB of HBM per device.

v0:
```python
import jax
import jax.numpy as jnp
from jax import lax
from jax.sharding import PartitionSpec as P


def per_device(gradient, feedback, right_initial):
    highest_precision_mode = lax.Precision.HIGHEST
    replicas = lax.axis_size("dp")
    merged_gradient = gradient[0].astype(jnp.float32) + feedback[0]
    left_partial = jnp.einsum(
        "lqg,lgh->lqh", merged_gradient, right_initial, precision=highest_precision_mode
    )
    p_full = lax.psum(left_partial, ("dp", "mp")) / replicas
    gram_matrix = jnp.einsum("mrk,mrl->mkl", p_full, p_full, precision=highest_precision_mode)
    factor_low = jnp.linalg.cholesky(gram_matrix)
    left_orthonormal = lax.linalg.triangular_solve(
        factor_low, p_full, left_side=False, lower=True, transpose_a=True
    )
    right_partial = jnp.einsum(
        "djs,djp->dsp", merged_gradient, left_orthonormal, precision=highest_precision_mode
    )
    right_averaged = lax.psum(right_partial, "dp") / replicas
    decoded = jnp.einsum(
        "gws,gos->gwo", left_orthonormal, right_averaged, precision=highest_precision_mode
    )
    carried = (merged_gradient - decoded)[None]
    return (decoded, carried)


def solution(mesh):
    placed = (P("dp", None, None, "mp"), P("dp", None, None, "mp"), P(None, "mp", None))
    return jax.shard_map(
        per_device,
        mesh=mesh,
        in_specs=placed,
        out_specs=(P(None, None, "mp"), P("dp", None, None, "mp")),
        check_vma=False,
    )
```

profile of v0, /device:TPU:1, one launch (start us, length us, event | category | flops | bytes accessed | tf_op | source)
XLA Modules:
  0.0 389.6 jit_solution(17809004107390279002)
XLA Ops:
  7.2 0.0 copy-start
  7.2 0.0 all-reduce.2.cloned.1.call-start
  7.3 1.1 copy-done
  8.3 0.0 copy-start.2
  8.4 4.9 %fusion.2 = f32[2,96,32]{1,2,0:T(8,128)S(1)} fusion(f32[2,3584,32]{1,2,0:T(8,128)S(1)} %copy-done, f32[1,2,96,3584]{3,2,1,0:T(8,128)} %param.4, bf16[1,2,96,3584]{3,2,1,0:T(8,128)(2,1)} %param.3), kind=kOutput, calls=%fused_computation.3 | convolution fusion | flops 265617408 | bytes 5070848 | tf_op jit(solution)/shard_map/lqg,lgh->lqh/dot_general | solution.py:11
  13.2 81.5 %psum.14 = f32[2,96,32]{1,2,0:T(8,128)S(1)} all-reduce(f32[2,96,32]{1,2,0:T(8,128)S(1)} %fusion.2), channel_id=1, replica_groups=mesh['dp'=32,'mp'=8] {'dp','mp'}, use_global_device_ids=true, to_apply=%region_0.0 | all-reduce | flops 6144 | bytes 49152 | tf_op jit(solution)/shard_map/psum | solution.py:14
  94.7 0.2 fusion.12
  94.9 0.1 copy.7
  95.0 5.9 %custom-call.7 = f32[2,32,32]{2,1,0:T(8,128)S(1)} custom-call(f32[2,32,32]{2,1,0:T(8,128)S(1)} %fusion.10), custom_call_target="Cholesky" | custom-call | tf_op jit(solution)/shard_map/jit(cholesky)/cholesky | solution.py:16
  100.9 0.1 compare_reduce_fusion
  101.0 0.1 select_bitcast_fusion
  101.1 4.9 %custom-call.8 = f32[2,1,32,32]{2,3,1,0:T(8,128)S(1)} custom-call(f32[2,1,32,32]{3,2,1,0:T(8,128)S(1)} %select_bitcast_fusion), custom_call_target="InvertDiagBlocksLowerTriangular" | custom-call | tf_op jit(solution)/shard_map/triangular_solve | solution.py:17
  106.0 0.3 fusion.8
  106.3 0.0 copy-done.2
  106.3 4.5 %fusion = f32[2,3584,32]{1,2,0:T(8,128)} fusion(f32[2,96,32]{1,2,0:T(8,128)S(1)} %fusion.8, f32[1,2,96,3584]{3,2,1,0:T(8,128)} %param.4, bf16[1,2,96,3584]{3,2,1,0:T(8,128)(2,1)S(1)} %copy-done.2), kind=kOutput, calls=%fused_computation.1 | convolution fusion | flops 265617408 | bytes 5070848 | tf_op jit(solution)/shard_map/djs,djp->dsp/dot_general | solution.py:20
  110.8 0.0 all-reduce.2.cloned.1.call-update
  110.8 265.8 %all-reduce.2.cloned.1.call-done = f32[2,3584,32]{1,2,0:T(8,128)} async-done(((f32[2,3584,32]{1,2,0:T(8,128)}), f32[2,3584,32]{1,2,0:T(8,128)}) %all-reduce.2.cloned.1.call-update) | async-done | bytes 917520 | tf_op jit(solution)/shard_map/psum | solution.py:23
  376.6 0.0 copy-start.1
  376.6 3.7 fusion.5
  380.3 0.0 copy-done.1
  380.3 0.0 copy-start.3
  380.3 2.4 fusion.4
  382.8 0.0 copy-done.3
  (4 shorter events, 0.1 us)
Async XLA Ops:
  7.2 1.2 copy-start
  7.2 369.5 %all-reduce.2.cloned.1.call-start = ((), (), s32[]{:S(2)}) async-start(), calls=%async_computation | async-start | bytes 1835008 | tf_op jit(solution)/shard_map/psum | solution.py:23
  8.3 97.9 %copy-start.2 = (bf16[1,2,96,3584]{3,2,1,0:T(8,128)(2,1)S(1)}, bf16[1,2,96,3584]{3,2,1,0:T(8,128)(2,1)}, u32[]{:S(2)}) copy-start(bf16[1,2,96,3584]{3,2,1,0:T(8,128)(2,1)} %param.3) | copy-start | bytes 4128772
  376.6 3.7 copy-start.1
  380.3 2.4 copy-start.3
Sparse Core Ops, SparseCore 0:
  110.9 265.6 all-reduce.1
where the time goes:
time: 391 us; the launch traced here: 390 us
  waiting for transfers between devices  266 us (68%)
  blocking collectives  81.5 us (21%)
  between operations  14.1 us (4%)
  other arithmetic  13.5 us (3%)
  matrix products  13.5 us (3%)
    psum x1, waiting for transfers between devices, per_device(): right_averaged = lax.psum(right_partial, 'dp') / replicas  266 us
    psum x1, blocking collectives, per_device(): p_full = lax.psum(left_partial, ('dp', 'mp')) / replicas  81.5 us
  transfers between devices with their start and end apart: 1, of which 1 were waited for; matrix products, arithmetic and copies ran while one was open for 0% of the time, Pallas kernels for 0%

commit v1 on v0

v1 whole, which is shorter than its diff:
```python
import functools

import jax
import jax.numpy as jnp
from jax import lax
from jax.experimental import pallas as pl
from jax.experimental.pallas import tpu as pltpu
from jax.sharding import PartitionSpec as P

MESH = pl.DeviceIdType.MESH
F32 = jnp.float32
BF16 = jnp.bfloat16
MATS, ROWS, RANK, COLS = 2, 96, 32, 3584
WIDTH = 896
HALF = ROWS // 2
REPLICAS = 32
VMEM_BYTES = 48 << 20


def split(a):
    hi = a.astype(BF16)
    return hi, (a - hi.astype(F32)).astype(BF16)


def dot(a, b, contract):
    return lax.dot_general(a, b, ((contract[0], contract[1]), ((), ())), preferred_element_type=F32)


def exact(a, b, contract):
    return lax.dot_general(
        a, b, ((contract[0], contract[1]), ((), ())), precision=lax.Precision.HIGHEST, preferred_element_type=F32
    )


def left_times_inverse(p_t):
    gram = exact(p_t, p_t, ((1,), (1,)))
    row = lax.broadcasted_iota(jnp.int32, (RANK, RANK), 0)
    col = lax.broadcasted_iota(jnp.int32, (RANK, RANK), 1)
    eye = jnp.where(row == col, 1.0, 0.0).astype(F32)
    inv = eye
    for k in range(RANK - 1):
        scale = 1.0 / gram[k : k + 1, k : k + 1]
        g_row = gram[k : k + 1, :] * scale
        i_row = inv[k : k + 1, :] * scale
        factor = jnp.where(row[:, 0:1] > k, gram[:, k : k + 1], 0.0)
        gram = gram - factor * g_row
        inv = inv - factor * i_row
    diag = jnp.sum(gram * eye, axis=1, keepdims=True)
    l_inv = inv * lax.rsqrt(diag)
    orth_t = exact(l_inv, p_t, ((1,), (0,)))
    return exact(l_inv, orth_t, ((0,), (0,)))


def reduce_kernel(
    g_hbm, f_hbm, r_hbm, comb, q_all, w_out,
    g_buf, f_buf, r_buf, c_recv, s_buf, r1, r2, p_own, p_core, p_y, p_x, p_z, p_full, q_part, z_part,
    load_sem, cs_sem, cr_sem, ss_sem, sr_sem, ps_sem, pr_sem, zs_sem, zr_sem, as_sem, ar_sem,
):
    d = lax.axis_index("dp")
    m = lax.axis_index("mp")
    zl, y, c = d // 8, (d // 2) % 4, d % 2
    x, zh = m // 2, m % 2
    z = zh * 4 + zl

    def at(zl_=zl, y_=y, c_=c, x_=x, zh_=zh):
        return (zl_ * 8 + y_ * 2 + c_, x_ * 2 + zh_)

    def z_peer(k):
        to = (z + k) % 8
        return at(zl_=to % 4, zh_=to // 4)

    core_peer = at(c_=1 - c)
    y_next, y_prev = (y + 1) % 4, (y + 3) % 4
    y_far = (y + 2) % 4
    y_peers = [at(y_=(y + k) % 4) for k in (1, 2, 3)]
    x_peers = [at(x_=(x + k) % 4) for k in (1, 2, 3)]
    z_peers = [z_peer(k) for k in range(1, 8)]

    sends = []

    def remote(src, dst, ssem, rsem, to):
        return pltpu.make_async_remote_copy(
            src_ref=src, dst_ref=dst, send_sem=ssem, recv_sem=rsem, device_id=to, device_id_type=MESH
        )

    def send(src, dst, ssem, rsem, to):
        copy = remote(src, dst, ssem, rsem, to)
        copy.start()
        sends.append(copy)

    def landed(dst, ssem, rsem):
        remote(dst, dst, ssem, rsem, core_peer).wait_recv()

    barrier = pltpu.get_barrier_semaphore()
    peers = [core_peer] + y_peers + x_peers + z_peers
    for to in peers:
        pl.semaphore_signal(barrier, inc=1, device_id=to, device_id_type=MESH)

    def chunk_cols(cc, yy):
        return pl.ds(pl.multiple_of((2 * cc + yy % 2) * WIDTH, 128), WIDTH)

    loads = []
    order = [(which, yy) for which in (0, 1) for yy in range(4)]
    for i, (which, yy) in enumerate(order):
        cc = 1 - c if which == 0 else c
        cols = chunk_cols(cc, yy)
        mat = yy // 2
        copies = [
            pltpu.make_async_copy(f_hbm.at[0, mat, :, cols], f_buf.at[i], load_sem.at[0, i]),
            pltpu.make_async_copy(g_hbm.at[0, mat, :, cols], g_buf.at[i], load_sem.at[1, i]),
            pltpu.make_async_copy(r_hbm.at[mat, :, cols], r_buf.at[i], load_sem.at[2, i]),
        ]
        for copy in copies:
            copy.start()
        loads.append(copies)

    p_sum = [jnp.zeros((2 * RANK, ROWS), F32) for _ in range(MATS)]
    for i, (which, yy) in enumerate(order):
        cc = 1 - c if which == 0 else c
        for copy in loads[i]:
            copy.wait()
        both = g_buf[i].astype(F32) + f_buf[i]
        comb[cc, yy] = both
        if i == 0:
            pl.semaphore_wait(barrier, len(peers))
        if which == 0:
            send(comb.at[cc, yy], c_recv.at[yy], cs_sem.at[yy], cr_sem.at[yy], core_peer)
        hi, lo = split(both)
        right = jnp.concatenate(split(r_buf[i]), axis=0)
        mat = yy // 2
        p_sum[mat] += dot(right, hi, ((1,), (1,))) + dot(right, lo, ((1,), (1,)))

    p_own[...] = jnp.zeros(p_own.shape, F32)
    for mat in range(MATS):
        p_own[mat, :, 0:ROWS] = p_sum[mat][:RANK] + p_sum[mat][RANK:]
    send(p_own.at[1 - c], p_core, ps_sem.at[0], pr_sem.at[0], core_peer)
    landed(p_core, ps_sem.at[0], pr_sem.at[0])
    p_y[y] = p_own[c] + p_core[...]
    for k, to in enumerate(y_peers):
        send(p_y.at[y], p_y.at[y], ps_sem.at[1 + k], pr_sem.at[1 + y], to)

    for yy in range(4):
        landed(c_recv.at[yy], cs_sem.at[yy], cr_sem.at[yy])
        s_buf[yy] = comb[c, yy] + c_recv[yy]
    top, low = pl.ds(0, HALF), pl.ds(HALF, HALF)
    to_next, to_prev = at(y_=y_next), at(y_=y_prev)
    send(s_buf.at[y_far, top], r1.at[0], ss_sem.at[0], sr_sem.at[0], to_next)
    send(s_buf.at[y_far, low], r1.at[1], ss_sem.at[1], sr_sem.at[1], to_prev)
    send(s_buf.at[y_next, low], r2.at[0], ss_sem.at[2], sr_sem.at[2], to_next)
    send(s_buf.at[y_prev, top], r2.at[1], ss_sem.at[3], sr_sem.at[3], to_prev)

    for k in (1, 2, 3):
        src = (y + k) % 4
        landed(p_y.at[src], ps_sem.at[0], pr_sem.at[1 + src])
    p_x[x] = (p_y[0] + p_y[1]) + (p_y[2] + p_y[3])
    for k, to in enumerate(x_peers):
        send(p_x.at[x], p_x.at[x], ps_sem.at[4 + k], pr_sem.at[5 + x], to)

    landed(r1.at[0], ss_sem.at[0], sr_sem.at[0])
    s_buf[y_next, top] += r1[0]
    send(s_buf.at[y_next, top], r2.at[2], ss_sem.at[4], sr_sem.at[4], to_next)
    landed(r1.at[1], ss_sem.at[1], sr_sem.at[1])
    s_buf[y_prev, low] += r1[1]
    send(s_buf.at[y_prev, low], r2.at[3], ss_sem.at[5], sr_sem.at[5], to_prev)

    for k in (1, 2, 3):
        src = (x + k) % 4
        landed(p_x.at[src], ps_sem.at[0], pr_sem.at[5 + src])
    p_z[z] = (p_x[0] + p_x[1]) + (p_x[2] + p_x[3])
    for k, to in enumerate(z_peers):
        send(p_z.at[z], p_z.at[z], ps_sem.at[7 + k], pr_sem.at[9 + z], to)
    for k in range(1, 8):
        src = (z + k) % 8
        landed(p_z.at[src], ps_sem.at[0], pr_sem.at[9 + src])
    total = ((p_z[0] + p_z[1]) + (p_z[2] + p_z[3])) + ((p_z[4] + p_z[5]) + (p_z[6] + p_z[7]))
    p_full[c] = total * (1.0 / REPLICAS)
    send(p_full.at[c], p_full.at[c], ps_sem.at[14], pr_sem.at[17], core_peer)

    for i in range(2):
        landed(r2.at[i], ss_sem.at[0], sr_sem.at[2 + i])
        landed(r2.at[2 + i], ss_sem.at[0], sr_sem.at[4 + i])
    chunk_top = (s_buf[y, top] + r2[1]) + r2[2]
    chunk_low = (s_buf[y, low] + r2[0]) + r2[3]
    landed(p_full.at[1 - c], ps_sem.at[0], pr_sem.at[17])

    left = jnp.concatenate(split(p_full[y // 2][:, :ROWS]), axis=0)
    hi, lo = split(jnp.concatenate([chunk_top, chunk_low], axis=0))
    prod = dot(left, hi, ((1,), (0,))) + dot(left, lo, ((1,), (0,)))
    q_part[...] = (prod[:RANK] + prod[RANK:]).reshape(4, 8, WIDTH)
    for k in (1, 2, 3):
        to = (zl + k) % 4
        send(q_part.at[to], z_part.at[zl], zs_sem.at[k], zr_sem.at[zl], at(zl_=to))
    z_part[zl] = q_part[zl]

    for mat in range(MATS):
        w_out[mat] = left_times_inverse(p_full[mat][:, :ROWS]) * (1.0 / REPLICAS)

    for k in (1, 2, 3):
        src = (zl + k) % 4
        landed(z_part.at[src], zs_sem.at[0], zr_sem.at[src])
    q_all[c, y, zl] = (z_part[0] + z_part[1]) + (z_part[2] + z_part[3])

    for k in (1, 2, 3):
        to = (zl + k) % 4
        send(q_all.at[c, y, zl], q_all.at[c, y, zl], as_sem.at[k], ar_sem.at[zl], at(zl_=to))
    for k in (1, 2, 3):
        src = (zl + k) % 4
        landed(q_all.at[c, y, src], as_sem.at[0], ar_sem.at[src])
    send(q_all.at[c, y], q_all.at[c, y], as_sem.at[4], ar_sem.at[4], to_next)
    send(q_all.at[c, y], q_all.at[c, y], as_sem.at[5], ar_sem.at[5], to_prev)
    send(q_all.at[c, y], q_all.at[c, y], as_sem.at[6], ar_sem.at[8], core_peer)
    first, second = pl.ds(0, 2), pl.ds(2, 2)
    landed(q_all.at[c, y_prev], as_sem.at[0], ar_sem.at[4])
    send(q_all.at[c, y_prev, first], q_all.at[c, y_prev, first], as_sem.at[7], ar_sem.at[6], to_next)
    send(q_all.at[c, y_prev], q_all.at[c, y_prev], as_sem.at[8], ar_sem.at[9], core_peer)
    landed(q_all.at[c, y_next], as_sem.at[0], ar_sem.at[5])
    send(q_all.at[c, y_next, second], q_all.at[c, y_next, second], as_sem.at[9], ar_sem.at[7], to_prev)
    send(q_all.at[c, y_next], q_all.at[c, y_next], as_sem.at[10], ar_sem.at[10], core_peer)
    landed(q_all.at[c, y_far, first], as_sem.at[0], ar_sem.at[6])
    landed(q_all.at[c, y_far, second], as_sem.at[0], ar_sem.at[7])
    send(q_all.at[c, y_far], q_all.at[c, y_far], as_sem.at[11], ar_sem.at[11], core_peer)
    for i, yy in enumerate((y, y_prev, y_next, y_far)):
        landed(q_all.at[1 - c, yy], as_sem.at[0], ar_sem.at[8 + i])
    for copy in sends:
        copy.wait_send()


def decode_kernel(comb, q_all, w_ref, decoded, carried, d_buf, c_buf, sem):
    left = []
    for mat in range(MATS):
        hi, lo = split(w_ref[mat].T)
        left.append(jnp.concatenate([hi, lo, hi, lo], axis=1))
    copies = []
    for i in range(8):
        cc, yy = i // 4, i % 4
        mat, cols = yy // 2, pl.ds((2 * cc + yy % 2) * WIDTH, WIDTH)
        hi, lo = split(q_all[cc, yy].reshape(RANK, WIDTH))
        out = dot(left[mat], jnp.concatenate([hi, hi, lo, lo], axis=0), ((1,), (0,)))
        d_buf[i] = out
        copies.append(pltpu.make_async_copy(d_buf.at[i], decoded.at[mat, :, cols], sem.at[0, i]))
        copies[-1].start()
        c_buf[i] = comb[cc, yy] - out
        copies.append(pltpu.make_async_copy(c_buf.at[i], carried.at[0, mat, :, cols], sem.at[1, i]))
        copies[-1].start()
    for copy in copies:
        copy.wait()


def per_device(gradient, feedback, right_initial):
    right_t = jnp.swapaxes(right_initial, 1, 2)
    vmem = pl.BlockSpec(memory_space=pltpu.VMEM)
    hbm = pl.BlockSpec(memory_space=pltpu.HBM)
    dma = pltpu.SemaphoreType.DMA
    comb, q_all, w = pl.pallas_call(
        reduce_kernel,
        name="reduce",
        out_shape=(
            jax.ShapeDtypeStruct((2, 4, ROWS, WIDTH), F32),
            jax.ShapeDtypeStruct((2, 4, 4, 8, WIDTH), F32),
            jax.ShapeDtypeStruct((MATS, RANK, ROWS), F32),
        ),
        in_specs=[hbm] * 3,
        out_specs=(vmem, vmem, vmem),
        scratch_shapes=[
            pltpu.VMEM((8, ROWS, WIDTH), BF16),
            pltpu.VMEM((8, ROWS, WIDTH), F32),
            pltpu.VMEM((8, RANK, WIDTH), F32),
            pltpu.VMEM((4, ROWS, WIDTH), F32),
            pltpu.VMEM((4, ROWS, WIDTH), F32),
            pltpu.VMEM((2, HALF, WIDTH), F32),
            pltpu.VMEM((4, HALF, WIDTH), F32),
            pltpu.VMEM((MATS, RANK, 128), F32),
            pltpu.VMEM((RANK, 128), F32),
            pltpu.VMEM((4, RANK, 128), F32),
            pltpu.VMEM((4, RANK, 128), F32),
            pltpu.VMEM((8, RANK, 128), F32),
            pltpu.VMEM((MATS, RANK, 128), F32),
            pltpu.VMEM((4, 8, WIDTH), F32),
            pltpu.VMEM((4, 8, WIDTH), F32),
            dma((3, 8)),
            dma((4,)),
            dma((4,)),
            dma((6,)),
            dma((6,)),
            dma((15,)),
            dma((18,)),
            dma((4,)),
            dma((4,)),
            dma((12,)),
            dma((12,)),
        ],
        compiler_params=pltpu.CompilerParams(
            collective_id=0, has_side_effects=True, vmem_limit_bytes=VMEM_BYTES
        ),
    )(gradient, feedback, right_t)
    return pl.pallas_call(
        decode_kernel,
        name="decode",
        out_shape=(
            jax.ShapeDtypeStruct((MATS, ROWS, COLS), F32),
            jax.ShapeDtypeStruct((1, MATS, ROWS, COLS), F32),
        ),
        in_specs=[vmem] * 3,
        out_specs=(hbm, hbm),
        scratch_shapes=[
            pltpu.VMEM((8, ROWS, WIDTH), F32),
            pltpu.VMEM((8, ROWS, WIDTH), F32),
            dma((2, 8)),
        ],
        compiler_params=pltpu.CompilerParams(vmem_limit_bytes=VMEM_BYTES),
    )(comb, q_all, w)


def solution(mesh):
    placed = (P("dp", None, None, "mp"), P("dp", None, None, "mp"), P(None, "mp", None))
    return jax.shard_map(
        per_device,
        mesh=mesh,
        in_specs=placed,
        out_specs=(P(None, None, "mp"), P("dp", None, None, "mp")),
        check_vma=False,
    )
```

time: 391 us -> 53.9 us (0.14)
  waiting for transfers between devices: 266 us -> 0 us
  blocking collectives: 81.5 us -> 0 us
  Pallas kernels: 0 us -> 50.6 us
  matrix products: 13.5 us -> 0 us
  other arithmetic: 13.5 us -> 0 us
  between operations: 14.1 us -> 0.65 us
    psum x1 -> x0, waiting for transfers between devices: 266 us -> none  [per_device(): right_averaged = lax.psum(right_partial, 'dp') / replicas]
    psum x1 -> x0, blocking collectives: 81.5 us -> none  [per_device(): p_full = lax.psum(left_partial, ('dp', 'mp')) / replicas]
    pallas_call x0 -> x2, Pallas kernels: none -> 50.6 us  [the longest x1 47.7 us: per_device(): pl.pallas_call(reduce_kernel, name='reduce', out_shape=(jax.ShapeDtypeStr...]
    dot_general x4 -> x0, matrix products: 13.2 us -> none  [the longest x1 4.86 us: per_device(): jnp.einsum('lqg,lgh->lqh', merged_gradient, right_initial, precision=high...]
    another operation x7 -> x0, other arithmetic: 11 us -> none  [the longest x4 6.03 us: per_device(): factor_low = jnp.linalg.cholesky(gram_matrix)]
  transfers between devices with their start and end apart: 1 -> 0, of which waited for: 1 -> 0; matrix products, arithmetic and copies ran while one was open for 0% -> 0% of each run, Pallas kernels for 0% -> 0%
where the time goes in v1:
time: 53.9 us; the launch traced here: 53.7 us
  Pallas kernels  50.6 us (94%)
  local copies, waits for them, and re-layouts  2.51 us (5%)
  between operations  0.65 us (1%)
    pallas_call x1, Pallas kernels, per_device(): pl.pallas_call(reduce_kernel, name='reduce', out_shape=(jax.ShapeDtypeStr...  47.7 us
    pallas_call x1, Pallas kernels, per_device(): pl.pallas_call(decode_kernel, name='decode', out_shape=(jax.ShapeDtypeStr...  2.9 us
    unnamed x4, local copies, waits for them, and re-layouts  2.51 us

profile of v1, /device:TPU:1, one launch (start us, length us, event | category | flops | bytes accessed | tf_op | source)
XLA Modules:
  0.0 53.7 jit_solution(6414265464216640863)
XLA Ops:
  0.6 0.0 copy-start
  0.6 1.3 %copy-done = bf16[1,2,96,3584]{3,2,1,0:T(8,128)(2,1)S(1)} copy-done((bf16[1,2,96,3584]{3,2,1,0:T(8,128)(2,1)S(1)}, bf16[1,2,96,3584]{3,2,1,0:T(8,128)(2,1)}, u32[]{:S(2)}) %copy-start) | copy-done | bytes 1376280
  2.0 0.0 copy-start.1
  2.0 1.2 %copy-done.1 = f32[2,3584,32]{1,2,0:T(8,128)S(1)} copy-done((f32[2,3584,32]{1,2,0:T(8,128)S(1)}, f32[2,3584,32]{1,2,0:T(8,128)}, u32[]{:S(2)}) %copy-start.1) | copy-done | bytes 917528
  3.1 47.7 %reduce.1 = (f32[2,4,96,896]{3,2,1,0:T(8,128)S(1)}, f32[2,4,4,8,896]{4,3,2,1,0:T(8,128)S(1)}, f32[2,32,96]{2,1,0:T(8,128)S(1)}) custom-call(bf16[1,2,96,3584]{3,2,1,0:T(8,128)(2,1)S(1)} %copy-done, f32[1,2,96,3584]{3,2,1,0:T(8,128)} %f_hbm.1, f32[2,32,3584]{2,1,0:T(8,128)S(1)} %bitcast.1), custom_call_target="tpu_custom_call" | custom-call | tf_op jit(solution)/shard_map/reduce/pallas_call | solution.py:254
  50.8 2.9 %decode.1 = (f32[2,96,3584]{2,1,0:T(8,128)}, f32[1,2,96,3584]{3,2,1,0:T(8,128)}) custom-call(f32[2,4,96,896]{3,2,1,0:T(8,128)S(1)} %get-tuple-element.5.comb, f32[2,4,4,8,896]{4,3,2,1,0:T(8,128)S(1)} %get-tuple-element.6.q_all, f32[2,32,96]{2,1,0:T(8,128)S(1)} %get-tuple-element.7.w_ref), custom_call_target="tpu_custom_call" | custom-call | tf_op jit(solution)/shard_map/decode/pallas_call | solution.py:296
Async XLA Ops:
  0.6 1.3 %copy-start = (bf16[1,2,96,3584]{3,2,1,0:T(8,128)(2,1)S(1)}, bf16[1,2,96,3584]{3,2,1,0:T(8,128)(2,1)}, u32[]{:S(2)}) copy-start(bf16[1,2,96,3584]{3,2,1,0:T(8,128)(2,1)} %g_hbm.1) | copy-start | bytes 4128772
  2.0 1.2 %copy-start.1 = (f32[2,3584,32]{1,2,0:T(8,128)S(1)}, f32[2,3584,32]{1,2,0:T(8,128)}, u32[]{:S(2)}) copy-start(f32[2,3584,32]{1,2,0:T(8,128)} %param.5) | copy-start | bytes 2752516

commit v2 on v0

v2 whole, which is shorter than its diff:
```python
import functools

import jax
import jax.numpy as jnp
from jax import lax
from jax.experimental import pallas as pl
from jax.experimental.pallas import tpu as pltpu
from jax.sharding import PartitionSpec as P

MESH = pl.DeviceIdType.MESH
F32 = jnp.float32
BF16 = jnp.bfloat16
MATS, ROWS, RANK, COLS = 2, 96, 32, 3584
WIDTH = 896
HALF = ROWS // 2
REPLICAS = 32
SENDS = 64
VMEM_BYTES = 32 << 20


def split(a):
    hi = a.astype(BF16)
    return hi, (a - hi.astype(F32)).astype(BF16)


def dot(a, b, contract):
    return lax.dot_general(a, b, ((contract[0], contract[1]), ((), ())), preferred_element_type=F32)


def exact(a, b, contract):
    return lax.dot_general(
        a, b, ((contract[0], contract[1]), ((), ())), precision=lax.Precision.HIGHEST, preferred_element_type=F32
    )


def left_times_inverses(p_ts):
    row = lax.broadcasted_iota(jnp.int32, (RANK, RANK), 0)
    col = lax.broadcasted_iota(jnp.int32, (RANK, RANK), 1)
    eye = jnp.where(row == col, 1.0, 0.0).astype(F32)
    grams = [exact(p_t, p_t, ((1,), (1,))) for p_t in p_ts]
    invs = [eye for _ in p_ts]
    for k in range(RANK - 1):
        below = row > k
        for i, (gram, inv) in enumerate(zip(grams, invs)):
            scale = 1.0 / gram[k : k + 1, k : k + 1]
            factor = jnp.where(below, jnp.broadcast_to(gram[:, k : k + 1], (RANK, RANK)), 0.0)
            grams[i] = gram - factor * (gram[k : k + 1, :] * scale)
            invs[i] = inv - factor * (inv[k : k + 1, :] * scale)
    out = []
    for gram, inv, p_t in zip(grams, invs, p_ts):
        diag = jnp.sum(gram * eye, axis=1, keepdims=True)
        l_inv = inv * lax.rsqrt(diag)
        orth_t = exact(l_inv, p_t, ((1,), (0,)))
        out.append(exact(l_inv, orth_t, ((0,), (0,))))
    return out


def decode(left, q):
    hi, lo = split(q)
    return dot(left, jnp.concatenate([hi, hi, lo, lo], axis=0), ((1,), (0,)))


class Net:
    def __init__(self, send_sem, recv_sem):
        self.send_sem, self.recv_sem = send_sem, recv_sem
        self.sent, self.due, self.last = [], {}, []

    def copy(self, src, dst, i, j, to):
        return pltpu.make_async_remote_copy(
            src_ref=src,
            dst_ref=dst,
            send_sem=self.send_sem.at[i],
            recv_sem=self.recv_sem.at[j],
            device_id=to,
            device_id_type=MESH,
        )

    def send(self, tag, src, dst, mine, to):
        i = len(self.sent)
        copy = self.copy(src, dst, i, i, to)
        copy.start()
        self.sent.append(copy)
        self.due.setdefault(tag, []).append((mine, i, to))

    def take(self, tag):
        for mine, i, to in self.due.pop(tag):
            self.copy(mine, mine, i, i, to).wait_recv()

    def at_end(self, step):
        self.last.append(step)

    def finish(self):
        for tag in list(self.due):
            self.take(tag)
        for copy in self.sent:
            copy.wait_send()
        for step in self.last:
            step()


def tree_sum(ref, n):
    terms = [ref[i] for i in range(n)]
    while len(terms) > 1:
        terms = [a + b for a, b in zip(terms[::2], terms[1::2])]
    return terms[0]


def reduce_kernel(
    g_hbm, f_hbm, r_hbm, comb, q_all, w_out, decoded, carried,
    g_buf, f_buf, r_buf, c_recv, s_buf, r1, r2, p_own, p_core, p_y, p_x, p_z, p_full, q_part, z_part,
    load_sem, send_sem, recv_sem,
):
    d = lax.axis_index("dp")
    m = lax.axis_index("mp")
    zl, y, c = d // 8, (d // 2) % 4, d % 2
    x, zh = m // 2, m % 2
    z = zh * 4 + zl
    net = Net(send_sem, recv_sem)
    send, take = net.send, net.take

    def at(zl_=zl, y_=y, c_=c, x_=x, zh_=zh):
        return (zl_ * 8 + y_ * 2 + c_, x_ * 2 + zh_)

    def y_at(k):
        return at(y_=(y + k) % 4)

    def x_at(k):
        return at(x_=(x + k) % 4)

    def z_at(k):
        to = (z + k) % 8
        return at(zl_=to % 4, zh_=to // 4)

    def zl_at(k):
        return at(zl_=(zl + k) % 4)

    core_peer = at(c_=1 - c)
    y_next, y_prev, y_far = (y + 1) % 4, (y + 3) % 4, (y + 2) % 4

    barrier = pltpu.get_barrier_semaphore()
    peers = [core_peer] + [f(k) for f, n in ((y_at, 4), (x_at, 4), (z_at, 8)) for k in range(1, n)]
    for to in peers:
        pl.semaphore_signal(barrier, inc=1, device_id=to, device_id_type=MESH)

    loads = []
    order = [(which, yy) for which in (0, 1) for yy in range(4)]
    for i, (which, yy) in enumerate(order):
        cc = 1 - c if which == 0 else c
        cols = pl.ds(pl.multiple_of((2 * cc + yy % 2) * WIDTH, 128), WIDTH)
        mat = yy // 2
        copies = [
            pltpu.make_async_copy(f_hbm.at[0, mat, :, cols], f_buf.at[i], load_sem.at[0, i]),
            pltpu.make_async_copy(g_hbm.at[0, mat, :, cols], g_buf.at[i], load_sem.at[1, i]),
            pltpu.make_async_copy(r_hbm.at[mat, :, cols], r_buf.at[i], load_sem.at[2, i]),
        ]
        for copy in copies:
            copy.start()
        loads.append(copies)
    p_sum = [jnp.zeros((2 * RANK, ROWS), F32) for _ in range(MATS)]
    for i, (which, yy) in enumerate(order):
        cc = 1 - c if which == 0 else c
        for copy in loads[i]:
            copy.wait()
        both = g_buf[i].astype(F32) + f_buf[i]
        comb[cc, yy] = both
        if i == 3:
            pl.semaphore_wait(barrier, len(peers))
            for part in range(4):
                send("core%d" % part, comb.at[cc, part], c_recv.at[part], c_recv.at[part], core_peer)
        hi, lo = split(both)
        right = jnp.concatenate(split(r_buf[i]), axis=0)
        mat = yy // 2
        p_sum[mat] += dot(right, hi, ((1,), (1,))) + dot(right, lo, ((1,), (1,)))

    p_own[...] = jnp.zeros(p_own.shape, F32)
    for mat in range(MATS):
        p_own[mat, :, 0:ROWS] = p_sum[mat][:RANK] + p_sum[mat][RANK:]
    send("p_core", p_own.at[1 - c], p_core, p_core, core_peer)
    take("p_core")
    p_y[y] = p_own[c] + p_core[...]
    for k in (1, 2, 3):
        send("p_y", p_y.at[y], p_y.at[y], p_y.at[(y + 4 - k) % 4], y_at(k))

    for yy in range(4):
        take("core%d" % yy)
        s_buf[yy] = comb[c, yy] + c_recv[yy]
    top, low = pl.ds(0, HALF), pl.ds(HALF, HALF)
    send("r_top", s_buf.at[y_far, top], r1.at[0], r1.at[0], y_at(1))
    send("r_low", s_buf.at[y_far, low], r1.at[1], r1.at[1], y_at(3))
    send("r_end", s_buf.at[y_next, low], r2.at[0], r2.at[0], y_at(1))
    send("r_end", s_buf.at[y_prev, top], r2.at[1], r2.at[1], y_at(3))

    take("p_y")
    p_x[x] = tree_sum(p_y, 4)
    for k in (1, 2, 3):
        send("p_x", p_x.at[x], p_x.at[x], p_x.at[(x + 4 - k) % 4], x_at(k))

    take("r_top")
    s_buf[y_next, top] += r1[0]
    send("r_end", s_buf.at[y_next, top], r2.at[2], r2.at[2], y_at(1))
    take("r_low")
    s_buf[y_prev, low] += r1[1]
    send("r_end", s_buf.at[y_prev, low], r2.at[3], r2.at[3], y_at(3))

    take("p_x")
    p_z[z] = tree_sum(p_x, 4)
    for k in range(1, 8):
        send("p_z", p_z.at[z], p_z.at[z], p_z.at[(z + 8 - k) % 8], z_at(k))
    take("p_z")
    p_full[c] = tree_sum(p_z, 8) * (1.0 / REPLICAS)
    send("p_full", p_full.at[c], p_full.at[c], p_full.at[1 - c], core_peer)
    take("p_full")
    take("r_end")
    chunk_top = (s_buf[y, top] + r2[1]) + r2[2]
    chunk_low = (s_buf[y, low] + r2[0]) + r2[3]

    left = jnp.concatenate(split(p_full[y // 2][:, :ROWS]), axis=0)
    hi, lo = split(jnp.concatenate([chunk_top, chunk_low], axis=0))
    prod = dot(left, hi, ((1,), (0,))) + dot(left, lo, ((1,), (0,)))
    q_part[...] = (prod[:RANK] + prod[RANK:]).reshape(2, 16, WIDTH)

    near = zl // 2
    far = 1 - near
    owner = (zl == 1) | (zl == 2)

    def to_owner(h):
        return net.copy(q_part.at[h], z_part.at[zl], SENDS + h, SENDS + zl, at(zl_=1 + h))

    def from_owner(k):
        mine = q_all.at[c, y, near]
        return net.copy(mine, mine, SENDS + 1 + k, SENDS + 4 + near, zl_at(k))

    def arrival(ref, i):
        return net.copy(ref, ref, SENDS, i, core_peer)

    for h in range(2):
        pl.when(zl != 1 + h)(to_owner(h).start)

    @net.at_end
    def _():
        for h in range(2):
            pl.when(zl != 1 + h)(to_owner(h).wait_send)

        @pl.when(owner)
        def _():
            for k in (1, 2, 3):
                from_owner(k).wait_send()

    for mat, left in enumerate(left_times_inverses([p_full[mat][:, :ROWS] for mat in range(MATS)])):
        hi, lo = split(left.T * (1.0 / REPLICAS))
        w_out[mat] = jnp.concatenate([hi, lo, hi, lo], axis=1)

    @pl.when(owner)
    def _():
        z_part[zl] = q_part[near]
        for k in (1, 2, 3):
            src = (zl + k) % 4
            arrival(z_part.at[src], SENDS + src).wait_recv()
        q_all[c, y, near] = tree_sum(z_part, 4)
        for k in (1, 2, 3):
            from_owner(k).start()

    @pl.when(jnp.logical_not(owner))
    def _():
        arrival(q_all.at[c, y, near], SENDS + 4 + near).wait_recv()

    def hand_on(tag, yy, half, yy_mine, core_mine, to):
        part = q_all.at[c, yy, half]
        send(tag, part, part, q_all.at[core_mine, yy_mine, half], to)

    for half, name in ((near, "near"), (far, "far")):
        if name == "far":
            arrival(q_all.at[c, y, far], SENDS + 4 + far).wait_recv()
        for k in (2, 1, 3):
            hand_on("%s%d" % (name, k), y, half, (y + 4 - k) % 4, c, y_at(k))
        hand_on(name + "core", y, half, y, 1 - c, core_peer)

    def decode_own(yy):
        out = decode(w_out[yy // 2], q_all[c, yy].reshape(RANK, WIDTH))
        decoded[yy] = out
        carried[yy] = comb[c, yy] - out

    for half, name in ((near, "near"), (far, "far")):
        for k in (1, 3, 2):
            take("%s%d" % (name, k))
            yy = (y + 4 - k) % 4
            hand_on(name + "core", yy, half, yy, 1 - c, core_peer)
        if name == "near":
            decode_own(y)
    for k in (1, 3, 2):
        decode_own((y + 4 - k) % 4)
    net.finish()


def write_kernel(comb, q_all, w_ref, own_decoded, own_carried, decoded, carried, d_buf, c_buf, sem):
    c = lax.axis_index("dp") % 2
    copies = []

    def write(i, cc, yy, d_ref, c_ref):
        cols = pl.ds(pl.multiple_of((2 * cc + yy % 2) * WIDTH, 128), WIDTH)
        for j, (ref, to) in enumerate(((d_ref, decoded.at[yy // 2, :, cols]), (c_ref, carried.at[0, yy // 2, :, cols]))):
            copies.append(pltpu.make_async_copy(ref, to, sem.at[j, i]))
            copies[-1].start()

    for yy in range(4):
        write(yy, c, yy, own_decoded.at[yy], own_carried.at[yy])
    for yy in range(4):
        out = decode(w_ref[yy // 2], q_all[1 - c, yy].reshape(RANK, WIDTH))
        d_buf[yy] = out
        c_buf[yy] = comb[1 - c, yy] - out
        write(4 + yy, 1 - c, yy, d_buf.at[yy], c_buf.at[yy])
    for copy in copies:
        copy.wait()


def reduce_call(gradient, feedback, right_initial, name="reduce", collective_id=0):
    right_t = jnp.swapaxes(right_initial, 1, 2)
    vmem = pl.BlockSpec(memory_space=pltpu.VMEM)
    hbm = pl.BlockSpec(memory_space=pltpu.HBM)
    dma = pltpu.SemaphoreType.DMA
    return pl.pallas_call(
        reduce_kernel,
        name=name,
        out_shape=(
            jax.ShapeDtypeStruct((2, 4, ROWS, WIDTH), F32),
            jax.ShapeDtypeStruct((2, 4, 2, 16, WIDTH), F32),
            jax.ShapeDtypeStruct((MATS, ROWS, 128), BF16),
            jax.ShapeDtypeStruct((4, ROWS, WIDTH), F32),
            jax.ShapeDtypeStruct((4, ROWS, WIDTH), F32),
        ),
        in_specs=[hbm] * 3,
        out_specs=(vmem,) * 5,
        scratch_shapes=[
            pltpu.VMEM((8, ROWS, WIDTH), BF16),
            pltpu.VMEM((8, ROWS, WIDTH), F32),
            pltpu.VMEM((8, RANK, WIDTH), F32),
            pltpu.VMEM((4, ROWS, WIDTH), F32),
            pltpu.VMEM((4, ROWS, WIDTH), F32),
            pltpu.VMEM((2, HALF, WIDTH), F32),
            pltpu.VMEM((4, HALF, WIDTH), F32),
            pltpu.VMEM((MATS, RANK, 128), F32),
            pltpu.VMEM((RANK, 128), F32),
            pltpu.VMEM((4, RANK, 128), F32),
            pltpu.VMEM((4, RANK, 128), F32),
            pltpu.VMEM((8, RANK, 128), F32),
            pltpu.VMEM((MATS, RANK, 128), F32),
            pltpu.VMEM((2, 16, WIDTH), F32),
            pltpu.VMEM((4, 16, WIDTH), F32),
            dma((3, 8)),
            dma((SENDS + 8,)),
            dma((SENDS + 8,)),
        ],
        compiler_params=pltpu.CompilerParams(
            collective_id=collective_id, has_side_effects=True, vmem_limit_bytes=VMEM_BYTES
        ),
    )(*(pltpu.with_memory_space_constraint(a, pltpu.HBM) for a in (gradient, feedback, right_t)))


def per_device(gradient, feedback, right_initial):
    vmem = pl.BlockSpec(memory_space=pltpu.VMEM)
    hbm = pl.BlockSpec(memory_space=pltpu.HBM)
    return pl.pallas_call(
        write_kernel,
        name="write",
        out_shape=(
            jax.ShapeDtypeStruct((MATS, ROWS, COLS), F32),
            jax.ShapeDtypeStruct((1, MATS, ROWS, COLS), F32),
        ),
        in_specs=[vmem] * 5,
        out_specs=(hbm, hbm),
        scratch_shapes=[
            pltpu.VMEM((4, ROWS, WIDTH), F32),
            pltpu.VMEM((4, ROWS, WIDTH), F32),
            pltpu.SemaphoreType.DMA((2, 8)),
        ],
        compiler_params=pltpu.CompilerParams(vmem_limit_bytes=VMEM_BYTES),
    )(*reduce_call(gradient, feedback, right_initial))


def solution(mesh):
    placed = (P("dp", None, None, "mp"), P("dp", None, None, "mp"), P(None, "mp", None))
    return jax.shard_map(
        per_device,
        mesh=mesh,
        in_specs=placed,
        out_specs=(P(None, None, "mp"), P("dp", None, None, "mp")),
        check_vma=False,
    )
```

time: 391 us -> 48 us (0.12)
  waiting for transfers between devices: 266 us -> 0 us
  blocking collectives: 81.5 us -> 0 us
  Pallas kernels: 0 us -> 47.2 us
  matrix products: 13.5 us -> 0 us
  other arithmetic: 13.5 us -> 0 us
  between operations: 14.1 us -> 0.64 us
    psum x1 -> x0, waiting for transfers between devices: 266 us -> none  [per_device(): right_averaged = lax.psum(right_partial, 'dp') / replicas]
    psum x1 -> x0, blocking collectives: 81.5 us -> none  [per_device(): p_full = lax.psum(left_partial, ('dp', 'mp')) / replicas]
    pallas_call x0 -> x2, Pallas kernels: none -> 47.2 us  [the longest x1 44.7 us: reduce_call(): pl.pallas_call(reduce_kernel, name=name, out_shape=(jax.ShapeDtypeStruct(...]
    dot_general x4 -> x0, matrix products: 13.2 us -> none  [the longest x1 4.86 us: per_device(): jnp.einsum('lqg,lgh->lqh', merged_gradient, right_initial, precision=high...]
    another operation x7 -> x0, other arithmetic: 11 us -> none  [the longest x4 6.03 us: per_device(): factor_low = jnp.linalg.cholesky(gram_matrix)]
  transfers between devices with their start and end apart: 1 -> 0, of which waited for: 1 -> 0; matrix products, arithmetic and copies ran while one was open for 0% -> 0% of each run, Pallas kernels for 0% -> 0%
where the time goes in v2:
time: 48 us; the launch traced here: 47.9 us
  Pallas kernels  47.2 us (98%)
  between operations  0.64 us (1%)
    pallas_call x1, Pallas kernels, reduce_call(): pl.pallas_call(reduce_kernel, name=name, out_shape=(jax.ShapeDtypeStruct(...  44.7 us
    pallas_call x1, Pallas kernels, per_device(): pl.pallas_call(write_kernel, name='write', out_shape=(jax.ShapeDtypeStruc...  2.57 us

profile of v2, /device:TPU:1, one launch (start us, length us, event | category | flops | bytes accessed | tf_op | source)
XLA Modules:
  0.0 47.9 jit_solution(17843682866190183027)
XLA Ops:
  0.6 44.7 %reduce.1 = (f32[2,4,96,896]{3,2,1,0:T(8,128)S(1)}, f32[2,4,2,16,896]{4,3,2,1,0:T(8,128)S(1)}, bf16[2,96,128]{2,1,0:T(8,128)(2,1)S(1)}, f32[4,96,896]{2,1,0:T(8,128)S(1)}, f32[4,96,896]{2,1,0:T(8,128)S(1)}) custom-call(bf16[1,2,96,3584]{3,2,1,0:T(8,128)(2,1)} %g_hbm.1, f32[1,2,96,3584]{3,2,1,0:T(8,128)} %f_hbm.1, f32[2,32,3584]{2,1,0:T(8,128)} %bitcast.1), custom_call_target="tpu_custom_call" | custom-call | tf_op jit(solution)/shard_map/reduce/pallas_call | solution.py:321
  45.3 2.6 %write.1 = (f32[2,96,3584]{2,1,0:T(8,128)}, f32[1,2,96,3584]{3,2,1,0:T(8,128)}) custom-call(f32[2,4,96,896]{3,2,1,0:T(8,128)S(1)} %get-tuple-element.7.comb, f32[2,4,2,16,896]{4,3,2,1,0:T(8,128)S(1)} %get-tuple-element.8.q_all, bf16[2,96,128]{2,1,0:T(8,128)(2,1)S(1)} %get-tuple-element.9.w_ref, f32[4,96,896]{2,1,0:T(8,128)S(1)} %get-tuple-element.10.own_decoded, ...), custom_call_target="tpu_custom_call" | custom-call | tf_op jit(solution)/shard_map/write/pallas_call | solution.py:362

commit v3 on v2

v3 whole, which is shorter than its diff:
```python
import jax
import jax.numpy as jnp
from jax import lax
from jax.experimental import pallas as pl
from jax.experimental.pallas import tpu as pltpu
from jax.sharding import PartitionSpec as P

MESH = pl.DeviceIdType.MESH
F32 = jnp.float32
BF16 = jnp.bfloat16
MATS, ROWS, RANK, COLS = 2, 96, 32, 3584
WIDTH = 896
PIECES = ((0, 512), (512, 384))
HALF = ROWS // 2
REPLICAS = 32
TAGS = 32
VMEM_BYTES = 32 << 20


def split(a):
    hi = a.astype(BF16)
    return hi, (a - hi.astype(F32)).astype(BF16)


def dot(a, b, contract):
    return lax.dot_general(a, b, ((contract[0], contract[1]), ((), ())), preferred_element_type=F32)


def exact(a, b, contract):
    return lax.dot_general(
        a, b, ((contract[0], contract[1]), ((), ())), precision=lax.Precision.HIGHEST, preferred_element_type=F32
    )


def left_times_inverse(p_t):
    gram = exact(p_t, p_t, ((1,), (1,)))
    row = lax.broadcasted_iota(jnp.int32, (RANK, RANK), 0)
    col = lax.broadcasted_iota(jnp.int32, (RANK, RANK), 1)
    eye = jnp.where(row == col, 1.0, 0.0).astype(F32)
    inv = eye
    for k in range(RANK - 1):
        scale = 1.0 / gram[k : k + 1, k : k + 1]
        factor = jnp.where(row > k, jnp.broadcast_to(gram[:, k : k + 1], (RANK, RANK)), 0.0)
        gram, inv = (a - factor * (a[k : k + 1, :] * scale) for a in (gram, inv))
    diag = jnp.sum(gram * eye, axis=1, keepdims=True)
    l_inv = inv * lax.rsqrt(diag)
    orth_t = exact(l_inv, p_t, ((1,), (0,)))
    return exact(l_inv, orth_t, ((0,), (0,)))


def decode(left, q):
    hi, lo = split(q)
    return dot(left, jnp.concatenate([hi, hi, lo, lo], axis=0), ((1,), (0,)))


class Net:
    def __init__(self, send_sem, recv_sem):
        self.send_sem, self.recv_sem = send_sem, recv_sem
        self.tags, self.due, self.sent, self.last = {}, {}, [], []

    def copy(self, tag, src, dst, to):
        return pltpu.make_async_remote_copy(
            src_ref=src,
            dst_ref=dst,
            send_sem=self.send_sem.at[0],
            recv_sem=self.recv_sem.at[self.tags.setdefault(tag, len(self.tags))],
            device_id=to,
            device_id_type=MESH,
        )

    def send(self, tag, src, dst, to):
        self.sent.append(self.copy(tag, src, dst, to))
        self.sent[-1].start()

    def landing(self, tag, ref, to):
        return self.copy(tag, ref, ref, to).wait_recv

    def expect(self, tag, ref, to):
        self.due[tag] = self.landing(tag, ref, to)

    def take(self, tag):
        self.due.pop(tag)()

    def at_end(self, step):
        self.last.append(step)

    def finish(self):
        for tag in list(self.due):
            self.take(tag)
        for copy in self.sent:
            copy.wait_send()
        for step in self.last:
            step()


def tree_sum(terms):
    while len(terms) > 1:
        terms = [a + b for a, b in zip(terms[::2], terms[1::2])]
    return terms[0]


def reduce_kernel(
    g_hbm, f_hbm, r_hbm, comb, q_all, w_out, decoded, carried,
    g_buf, f_buf, r_buf, c_recv, s_buf, r1, r2, p_own, p_core, p_mid, p_y, p_x, p_z, p_full, w_t, q_part, z_part,
    load_sem, send_sem, recv_sem,
):
    d = lax.axis_index("dp")
    m = lax.axis_index("mp")
    zl, y, c = d // 8, (d // 2) % 4, d % 2
    x, zh = m // 2, m % 2
    z = zh * 4 + zl
    net = Net(send_sem, recv_sem)
    send, take = net.send, net.take

    def at(zl_=zl, y_=y, c_=c, x_=x, zh_=zh):
        return (zl_ * 8 + y_ * 2 + c_, x_ * 2 + zh_)

    def y_at(k):
        return at(y_=(y + k) % 4)

    def x_at(k):
        return at(x_=(x + k) % 4)

    def z_at(k):
        to = (z + k) % 8
        return at(zl_=to % 4, zh_=to // 4)

    def zl_at(k):
        return at(zl_=(zl + k) % 4)

    core_peer = at(c_=1 - c)
    y_next, y_prev, y_far = (y + 1) % 4, (y + 3) % 4, (y + 2) % 4
    mat = y // 2

    pairs = [(1 - c, 1 - mat), (c, 1 - mat), (1 - c, mat), (c, mat)]
    loads = []
    for i, (cc, mm) in enumerate(pairs):
        cols = pl.ds(pl.multiple_of(cc * 2 * WIDTH, 128), 2 * WIDTH)
        loads.append(
            (
                pltpu.make_async_copy(f_hbm.at[0, mm, :, cols], f_buf.at[i], load_sem.at[i]),
                pltpu.make_async_copy(g_hbm.at[0, mm, :, cols], g_buf.at[i], load_sem.at[4 + i]),
            )
        )
    right_load = pltpu.make_async_copy(r_hbm, r_buf, load_sem.at[8])
    for copies in loads:
        for copy in copies:
            copy.start()
    right_load.start()

    barrier = pltpu.get_barrier_semaphore()
    peers = [core_peer] + [f(k) for f, n in ((y_at, 4), (x_at, 4), (z_at, 8)) for k in range(1, n)]
    for to in peers:
        pl.semaphore_signal(barrier, inc=1, device_id=to, device_id_type=MESH)
    p_own[...] = jnp.zeros(p_own.shape, F32)

    def combine(i, yy):
        cc = pairs[i][0]
        cols = pl.ds(pl.multiple_of(yy % 2 * WIDTH, 128), WIDTH)
        comb[cc, yy] = g_buf[i, :, cols].astype(F32) + f_buf[i, :, cols]

    def to_core(name, yy):
        send(name, comb.at[1 - c, yy], c_recv.at[yy], core_peer)
        net.expect(name, c_recv.at[yy], core_peer)

    def sum_cores(name, yy):
        take(name)
        s_buf[yy] = comb[c, yy] + c_recv[yy]

    def left_product(i, yy):
        hi, lo = split(comb[pairs[i][0], yy])
        cols = pl.ds(pl.multiple_of((2 * pairs[i][0] + yy % 2) * WIDTH, 128), WIDTH)
        right = jnp.concatenate(split(r_buf[yy // 2, :, cols]), axis=0)
        both = (dot(hi, right, ((1,), (1,))) + dot(lo, right, ((1,), (1,)))).T
        p_own[yy // 2, :, 0:ROWS] += both[:RANK] + both[RANK:]

    y_beside = mat * 2 + 1 - y % 2
    y_across = (1 - mat) * 2 + 1 - y % 2
    order = [(0, y_far), (1, y_far), (0, y_across), (1, y_across), (2, y_beside), (3, y_beside), (2, y), (3, y)]
    top, low = pl.ds(0, HALF), pl.ds(HALF, HALF)

    def wait_load(i):
        for copy in loads[i]:
            copy.wait()

    wait_load(0)
    combine(0, y_far)
    pl.semaphore_wait(barrier, len(peers))
    to_core("c_far", y_far)
    combine(0, y_across)
    to_core("c_across", y_across)
    wait_load(1)
    combine(1, y_far)
    combine(1, y_across)
    wait_load(2)
    combine(2, y_beside)
    to_core("c_beside", y_beside)
    combine(2, y)
    to_core("c_own", y)
    right_load.wait()
    for step in order[:3]:
        left_product(*step)
    sum_cores("c_far", y_far)
    send("r_top", s_buf.at[y_far, top], r1.at[0], y_at(1))
    send("r_low", s_buf.at[y_far, low], r1.at[1], y_at(3))
    net.expect("r_top", r1.at[0], y_at(1))
    net.expect("r_low", r1.at[1], y_at(3))
    wait_load(3)
    combine(3, y_beside)
    combine(3, y)
    for step in order[3:]:
        left_product(*step)

    ranks = pl.ds(pl.multiple_of(c * 16, 16), 16)
    send("p_core", p_own, p_core, core_peer)
    net.expect("p_core", p_core, core_peer)
    sum_cores("c_across", y_across)
    sum_cores("c_beside", y_beside)
    take("p_core")
    p_mid[...] = p_own[...] + p_core[...]
    for k in (2, 1, 3):
        send("p_y", p_mid.at[(y + k) % 4 // 2, ranks], p_y.at[y], y_at(k))
    net.expect("p_y", p_y.at[pl.ds(0, 3)], core_peer)
    p_y[y] = p_mid[mat, ranks]

    send("r_end", s_buf.at[y_next, low], r2.at[0], y_at(1))
    send("r_end", s_buf.at[y_prev, top], r2.at[1], y_at(3))
    net.expect("r_end", r2, core_peer)
    take("r_top")
    s_buf[y_next, top] += r1[0]
    send("r_end", s_buf.at[y_next, top], r2.at[2], y_at(1))
    take("r_low")
    s_buf[y_prev, low] += r1[1]
    send("r_end", s_buf.at[y_prev, low], r2.at[3], y_at(3))
    sum_cores("c_own", y)

    take("p_y")
    p_x[x] = tree_sum([p_y[i] for i in range(4)])
    for k in (2, 1, 3):
        send("p_x", p_x.at[x], p_x.at[x], x_at(k))
    net.expect("p_x", p_x.at[pl.ds(0, 3)], core_peer)
    take("p_x")
    p_z[z] = tree_sum([p_x[i] for i in range(4)])
    for k in (4, 3, 5, 2, 6, 1, 7):
        send("p_z", p_z.at[z], p_z.at[z], z_at(k))
    net.expect("p_z", p_z.at[pl.ds(0, 7)], core_peer)
    take("p_z")
    p_full[ranks] = tree_sum([p_z[i] for i in range(8)]) * (1.0 / REPLICAS)
    send("p_full", p_full.at[ranks], p_full.at[ranks], core_peer)
    net.expect("p_full", p_full.at[pl.ds(pl.multiple_of(16 - c * 16, 16), 16)], core_peer)
    take("p_full")
    take("r_end")
    s_buf[y, top] = (s_buf[y, top] + r2[1]) + r2[2]
    s_buf[y, low] = (s_buf[y, low] + r2[0]) + r2[3]

    near = zl // 2
    far = 1 - near
    owner = (zl == 1) | (zl == 2)

    def cols_of(piece):
        return pl.ds(*PIECES[piece])

    def to_owner(h, piece):
        cols = cols_of(piece)
        return net.copy("z_sum%d" % piece, q_part.at[h, :, cols], z_part.at[zl, :, cols], at(zl_=1 + h))

    def from_owner(h, k, piece):
        mine = q_all.at[c, y, h, :, cols_of(piece)]
        return net.copy("half%d%d" % (h, piece), mine, mine, zl_at(k))

    left = jnp.concatenate(split(p_full[:, :ROWS]), axis=0)
    for piece in range(2):
        cols = cols_of(piece)
        hi, lo = split(s_buf[y, :, cols])
        prod = dot(left, hi, ((1,), (0,))) + dot(left, lo, ((1,), (0,)))
        q_part[:, :, cols] = (prod[:RANK] + prod[RANK:]).reshape(2, 16, PIECES[piece][1])
        for h in range(2):
            pl.when(zl != 1 + h)(to_owner(h, piece).start)

    @net.at_end
    def _():
        for piece in range(2):
            for h in range(2):
                pl.when(zl != 1 + h)(to_owner(h, piece).wait_send)

        @pl.when(owner)
        def _():
            for piece in range(2):
                for k in (1, 2, 3):
                    from_owner(0, k, piece).wait_send()

    w_t[mat, :, 0:ROWS] = left_times_inverse(p_full[:, :ROWS]) * (1.0 / REPLICAS)
    send("w", w_t.at[mat], w_t.at[mat], y_at(2))
    net.expect("w", w_t.at[1 - mat], y_at(2))

    def hand_on(tag, yy, half, piece, to):
        part = q_all.at[c, yy, half, :, cols_of(piece)]
        send(tag, part, part, to)

    for half, name in ((near, "near"), (far, "far")):
        for piece in range(2):
            cols = cols_of(piece)
            landing = [net.landing("half%d%d" % (h, piece), q_all.at[c, y, h, :, cols], core_peer) for h in range(2)]

            def land(half=half, landing=landing):
                for h in range(2):
                    pl.when(half == h)(landing[h])

            if name == "far":
                land()
            else:

                @pl.when(owner)
                def _(piece=piece, cols=cols):
                    z_part[zl, :, cols] = q_part[near, :, cols]
                    net.landing("z_sum%d" % piece, z_part.at[pl.ds(0, 3), :, cols], core_peer)()
                    q_all[c, y, near, :, cols] = tree_sum([z_part[i, :, cols] for i in range(4)])
                    for h in range(2):

                        @pl.when(near == h)
                        def _():
                            for k in (1, 2, 3):
                                from_owner(h, k, piece).start()

                pl.when(jnp.logical_not(owner))(land)
            for k in (2, 1, 3):
                tag = "%s%d_%d" % (name, piece, k)
                hand_on(tag, y, half, piece, y_at(k))
                net.expect(tag, q_all.at[c, (y + 4 - k) % 4, half, :, cols], core_peer)
            hand_on("core", y, half, piece, core_peer)
    net.expect("core", q_all.at[1 - c], core_peer)

    def decode_own(yy):
        out = decode(w_out[yy // 2], q_all[c, yy].reshape(RANK, WIDTH))
        decoded[yy] = out
        carried[yy] = comb[c, yy] - out

    for half, name in ((near, "near"), (far, "far")):
        for piece in range(2):
            for k in (1, 3, 2):
                take("%s%d_%d" % (name, piece, k))
                hand_on("core", (y + 4 - k) % 4, half, piece, core_peer)
        if name == "near":
            take("w")
            for i in range(MATS):
                hi, lo = split(w_t[i, :, 0:ROWS].T)
                w_out[i] = jnp.concatenate([hi, lo, hi, lo], axis=1)
            decode_own(y)
    for k in (1, 3, 2):
        decode_own((y + 4 - k) % 4)
    net.finish()


def write_kernel(comb, q_all, w_ref, own_decoded, own_carried, decoded, carried, d_buf, c_buf, sem):
    c = lax.axis_index("dp") % 2
    copies = []

    def write(cc, yy, d_ref, c_ref):
        cols = pl.ds(pl.multiple_of((2 * cc + yy % 2) * WIDTH, 128), WIDTH)
        for ref, to in ((d_ref, decoded.at[yy // 2, :, cols]), (c_ref, carried.at[0, yy // 2, :, cols])):
            copies.append(pltpu.make_async_copy(ref, to, sem.at[0]))
            copies[-1].start()

    for yy in range(4):
        write(c, yy, own_decoded.at[yy], own_carried.at[yy])
    for yy in range(4):
        out = decode(w_ref[yy // 2], q_all[1 - c, yy].reshape(RANK, WIDTH))
        d_buf[yy] = out
        c_buf[yy] = comb[1 - c, yy] - out
        write(1 - c, yy, d_buf.at[yy], c_buf.at[yy])
    for copy in copies:
        copy.wait()


def reduce_call(gradient, feedback, right_initial, name="reduce", collective_id=0):
    right_t = jnp.swapaxes(right_initial, 1, 2)
    vmem = pl.BlockSpec(memory_space=pltpu.VMEM)
    hbm = pl.BlockSpec(memory_space=pltpu.HBM)
    dma = pltpu.SemaphoreType.DMA
    return pl.pallas_call(
        reduce_kernel,
        name=name,
        out_shape=(
            jax.ShapeDtypeStruct((2, 4, ROWS, WIDTH), F32),
            jax.ShapeDtypeStruct((2, 4, 2, 16, WIDTH), F32),
            jax.ShapeDtypeStruct((MATS, ROWS, 128), BF16),
            jax.ShapeDtypeStruct((4, ROWS, WIDTH), F32),
            jax.ShapeDtypeStruct((4, ROWS, WIDTH), F32),
        ),
        in_specs=[hbm] * 3,
        out_specs=(vmem,) * 5,
        scratch_shapes=[
            pltpu.VMEM((4, ROWS, 2 * WIDTH), BF16),
            pltpu.VMEM((4, ROWS, 2 * WIDTH), F32),
            pltpu.VMEM((MATS, RANK, COLS), F32),
            pltpu.VMEM((4, ROWS, WIDTH), F32),
            pltpu.VMEM((4, ROWS, WIDTH), F32),
            pltpu.VMEM((2, HALF, WIDTH), F32),
            pltpu.VMEM((4, HALF, WIDTH), F32),
            pltpu.VMEM((MATS, RANK, 128), F32),
            pltpu.VMEM((MATS, RANK, 128), F32),
            pltpu.VMEM((MATS, RANK, 128), F32),
            pltpu.VMEM((4, 16, 128), F32),
            pltpu.VMEM((4, 16, 128), F32),
            pltpu.VMEM((8, 16, 128), F32),
            pltpu.VMEM((RANK, 128), F32),
            pltpu.VMEM((MATS, RANK, 128), F32),
            pltpu.VMEM((2, 16, WIDTH), F32),
            pltpu.VMEM((4, 16, WIDTH), F32),
            dma((9,)),
            dma((1,)),
            dma((TAGS,)),
        ],
        compiler_params=pltpu.CompilerParams(
            collective_id=collective_id, has_side_effects=True, vmem_limit_bytes=VMEM_BYTES
        ),
    )(*(pltpu.with_memory_space_constraint(a, pltpu.HBM) for a in (gradient, feedback, right_t)))


def per_device(gradient, feedback, right_initial):
    vmem = pl.BlockSpec(memory_space=pltpu.VMEM)
    hbm = pl.BlockSpec(memory_space=pltpu.HBM)
    return pl.pallas_call(
        write_kernel,
        name="write",
        out_shape=(
            jax.ShapeDtypeStruct((MATS, ROWS, COLS), F32),
            jax.ShapeDtypeStruct((1, MATS, ROWS, COLS), F32),
        ),
        in_specs=[vmem] * 5,
        out_specs=(hbm, hbm),
        scratch_shapes=[
            pltpu.VMEM((4, ROWS, WIDTH), F32),
            pltpu.VMEM((4, ROWS, WIDTH), F32),
            pltpu.SemaphoreType.DMA((1,)),
        ],
        compiler_params=pltpu.CompilerParams(vmem_limit_bytes=VMEM_BYTES),
    )(*reduce_call(gradient, feedback, right_initial))


def solution(mesh):
    placed = (P("dp", None, None, "mp"), P("dp", None, None, "mp"), P(None, "mp", None))
    return jax.shard_map(
        per_device,
        mesh=mesh,
        in_specs=placed,
        out_specs=(P(None, None, "mp"), P("dp", None, None, "mp")),
        check_vma=False,
    )
```

time: 48 us -> 45 us (0.938)
  Pallas kernels: 47.2 us -> 44.3 us
    pallas_call x1, Pallas kernels: 44.7 us -> 41.8 us  [reduce_call(): pl.pallas_call(reduce_kernel, name=name, out_shape=(jax.ShapeDtypeStruct(...]
where the time goes in v3:
time: 45 us; the launch traced here: 44.9 us
  Pallas kernels  44.3 us (98%)
  between operations  0.64 us (1%)
    pallas_call x1, Pallas kernels, reduce_call(): pl.pallas_call(reduce_kernel, name=name, out_shape=(jax.ShapeDtypeStruct(...  41.8 us
    pallas_call x1, Pallas kernels, per_device(): pl.pallas_call(write_kernel, name='write', out_shape=(jax.ShapeDtypeStruc...  2.44 us

profile of v3, /device:TPU:1, one launch (start us, length us, event | category | flops | bytes accessed | tf_op | source)
XLA Modules:
  0.0 44.9 jit_solution(525220036219002335)
XLA Ops:
  0.6 41.8 %reduce.1 = (f32[2,4,96,896]{3,2,1,0:T(8,128)S(1)}, f32[2,4,2,16,896]{4,3,2,1,0:T(8,128)S(1)}, bf16[2,96,128]{2,1,0:T(8,128)(2,1)S(1)}, f32[4,96,896]{2,1,0:T(8,128)S(1)}, f32[4,96,896]{2,1,0:T(8,128)S(1)}) custom-call(bf16[1,2,96,3584]{3,2,1,0:T(8,128)(2,1)} %g_hbm.1, f32[1,2,96,3584]{3,2,1,0:T(8,128)} %f_hbm.1, f32[2,32,3584]{2,1,0:T(8,128)} %bitcast.1), custom_call_target="tpu_custom_call" | custom-call | tf_op jit(solution)/shard_map/reduce/pallas_call | solution.py:380
  42.5 2.4 %write.1 = (f32[2,96,3584]{2,1,0:T(8,128)}, f32[1,2,96,3584]{3,2,1,0:T(8,128)}) custom-call(f32[2,4,96,896]{3,2,1,0:T(8,128)S(1)} %get-tuple-element.7.comb, f32[2,4,2,16,896]{4,3,2,1,0:T(8,128)S(1)} %get-tuple-element.8.q_all, bf16[2,96,128]{2,1,0:T(8,128)(2,1)S(1)} %get-tuple-element.9.w_ref, f32[4,96,896]{2,1,0:T(8,128)S(1)} %get-tuple-element.10.own_decoded, ...), custom_call_target="tpu_custom_call" | custom-call | tf_op jit(solution)/shard_map/write/pallas_call | solution.py:423

commit v4 on v3

--- a/solution.py
+++ b/solution.py
@@ -10,10 +10,10 @@
 BF16 = jnp.bfloat16
 MATS, ROWS, RANK, COLS = 2, 96, 32, 3584
 WIDTH = 896
-PIECES = ((0, 512), (512, 384))
+PIECES = ((0, 256), (256, 256), (512, 256), (768, 128))
 HALF = ROWS // 2
 REPLICAS = 32
-TAGS = 32
+TAGS = 56
 VMEM_BYTES = 32 << 20
 
 
@@ -101,7 +101,7 @@
 
 def reduce_kernel(
     g_hbm, f_hbm, r_hbm, comb, q_all, w_out, decoded, carried,
-    g_buf, f_buf, r_buf, c_recv, s_buf, r1, r2, p_own, p_core, p_mid, p_y, p_x, p_z, p_full, w_t, q_part, z_part,
+    g_buf, f_buf, r_buf, c_recv, s_buf, r1, r2, p_own, p_y, p_x, p_z, p_full, w_t, q_part, z_part,
     load_sem, send_sem, recv_sem,
 ):
     d = lax.axis_index("dp")
@@ -143,16 +143,17 @@
             )
         )
     right_load = pltpu.make_async_copy(r_hbm, r_buf, load_sem.at[8])
+    right_load.start()
     for copies in loads:
         for copy in copies:
             copy.start()
-    right_load.start()
 
     barrier = pltpu.get_barrier_semaphore()
-    peers = [core_peer] + [f(k) for f, n in ((y_at, 4), (x_at, 4), (z_at, 8)) for k in range(1, n)]
+    peers = [core_peer] + [at(y_=(y + k) % 4, c_=1 - c) for k in (1, 2, 3)] + [f(k) for f, n in ((y_at, 4), (x_at, 4), (z_at, 8)) for k in range(1, n)]
     for to in peers:
         pl.semaphore_signal(barrier, inc=1, device_id=to, device_id_type=MESH)
     p_own[...] = jnp.zeros(p_own.shape, F32)
+    p_sums = {}
 
     def combine(i, yy):
         cc = pairs[i][0]
@@ -171,58 +172,57 @@
         hi, lo = split(comb[pairs[i][0], yy])
         cols = pl.ds(pl.multiple_of((2 * pairs[i][0] + yy % 2) * WIDTH, 128), WIDTH)
         right = jnp.concatenate(split(r_buf[yy // 2, :, cols]), axis=0)
-        both = (dot(hi, right, ((1,), (1,))) + dot(lo, right, ((1,), (1,)))).T
-        p_own[yy // 2, :, 0:ROWS] += both[:RANK] + both[RANK:]
+        both = dot(jnp.concatenate([hi, lo], axis=0), right, ((1,), (1,)))
+        p_sums.setdefault(i // 2, []).append(both[:ROWS] + both[ROWS:])
+
+    def left_sum(i):
+        both = tree_sum(p_sums[i]).T
+        p_own[mat if i else 1 - mat, :, 0:ROWS] = both[:RANK] + both[RANK:]
 
     y_beside = mat * 2 + 1 - y % 2
     y_across = (1 - mat) * 2 + 1 - y % 2
-    order = [(0, y_far), (1, y_far), (0, y_across), (1, y_across), (2, y_beside), (3, y_beside), (2, y), (3, y)]
     top, low = pl.ds(0, HALF), pl.ds(HALF, HALF)
 
     def wait_load(i):
         for copy in loads[i]:
             copy.wait()
 
-    wait_load(0)
-    combine(0, y_far)
-    pl.semaphore_wait(barrier, len(peers))
-    to_core("c_far", y_far)
-    combine(0, y_across)
-    to_core("c_across", y_across)
-    wait_load(1)
-    combine(1, y_far)
-    combine(1, y_across)
-    wait_load(2)
-    combine(2, y_beside)
-    to_core("c_beside", y_beside)
-    combine(2, y)
-    to_core("c_own", y)
     right_load.wait()
-    for step in order[:3]:
-        left_product(*step)
+    for i in range(4):
+        wait_load(i)
+        if i == 0:
+            pl.semaphore_wait(barrier, len(peers))
+        for name, yy in ((("far", y_far), ("across", y_across)), (("beside", y_beside), ("own", y)))[i // 2]:
+            combine(i, yy)
+            if i % 2 == 0:
+                to_core("c_" + name, yy)
+            left_product(i, yy)
+        if i % 2 == 1:
+            left_sum(i // 2)
+
+    ranks = pl.ds(pl.multiple_of(c * 16, 16), 16)
+    for k in (2, 1, 3, 0):
+        for same in ((0, 1) if k else (0,)):
+            cc = c if same else 1 - c
+            part = p_own.at[(y + k) % 4 // 2, pl.ds(pl.multiple_of(cc * 16, 16), 16)]
+            send("p_y", part, p_y.at[2 * y + c], at(y_=(y + k) % 4, c_=cc))
+    net.expect("p_y", p_y.at[pl.ds(0, 7)], core_peer)
+    p_y[2 * y + c] = p_own[mat, ranks]
+
     sum_cores("c_far", y_far)
     send("r_top", s_buf.at[y_far, top], r1.at[0], y_at(1))
     send("r_low", s_buf.at[y_far, low], r1.at[1], y_at(3))
     net.expect("r_top", r1.at[0], y_at(1))
     net.expect("r_low", r1.at[1], y_at(3))
-    wait_load(3)
-    combine(3, y_beside)
-    combine(3, y)
-    for step in order[3:]:
-        left_product(*step)
-
-    ranks = pl.ds(pl.multiple_of(c * 16, 16), 16)
-    send("p_core", p_own, p_core, core_peer)
-    net.expect("p_core", p_core, core_peer)
     sum_cores("c_across", y_across)
     sum_cores("c_beside", y_beside)
-    take("p_core")
-    p_mid[...] = p_own[...] + p_core[...]
+    sum_cores("c_own", y)
+
+    take("p_y")
+    p_x[x] = tree_sum([p_y[i] for i in range(8)])
     for k in (2, 1, 3):
-        send("p_y", p_mid.at[(y + k) % 4 // 2, ranks], p_y.at[y], y_at(k))
-    net.expect("p_y", p_y.at[pl.ds(0, 3)], core_peer)
-    p_y[y] = p_mid[mat, ranks]
-
+        send("p_x", p_x.at[x], p_x.at[x], x_at(k))
+    net.expect("p_x", p_x.at[pl.ds(0, 3)], core_peer)
     send("r_end", s_buf.at[y_next, low], r2.at[0], y_at(1))
     send("r_end", s_buf.at[y_prev, top], r2.at[1], y_at(3))
     net.expect("r_end", r2, core_peer)
@@ -232,13 +232,7 @@
     take("r_low")
     s_buf[y_prev, low] += r1[1]
     send("r_end", s_buf.at[y_prev, low], r2.at[3], y_at(3))
-    sum_cores("c_own", y)
-
-    take("p_y")
-    p_x[x] = tree_sum([p_y[i] for i in range(4)])
-    for k in (2, 1, 3):
-        send("p_x", p_x.at[x], p_x.at[x], x_at(k))
-    net.expect("p_x", p_x.at[pl.ds(0, 3)], core_peer)
+
     take("p_x")
     p_z[z] = tree_sum([p_x[i] for i in range(4)])
     for k in (4, 3, 5, 2, 6, 1, 7):
@@ -269,7 +263,7 @@
         return net.copy("half%d%d" % (h, piece), mine, mine, zl_at(k))
 
     left = jnp.concatenate(split(p_full[:, :ROWS]), axis=0)
-    for piece in range(2):
+    for piece in range(len(PIECES)):
         cols = cols_of(piece)
         hi, lo = split(s_buf[y, :, cols])
         prod = dot(left, hi, ((1,), (0,))) + dot(left, lo, ((1,), (0,)))
@@ -279,13 +273,13 @@
 
     @net.at_end
     def _():
-        for piece in range(2):
+        for piece in range(len(PIECES)):
             for h in range(2):
                 pl.when(zl != 1 + h)(to_owner(h, piece).wait_send)
 
         @pl.when(owner)
         def _():
-            for piece in range(2):
+            for piece in range(len(PIECES)):
                 for k in (1, 2, 3):
                     from_owner(0, k, piece).wait_send()
 
@@ -298,7 +292,7 @@
         send(tag, part, part, to)
 
     for half, name in ((near, "near"), (far, "far")):
-        for piece in range(2):
+        for piece in range(len(PIECES)):
             cols = cols_of(piece)
             landing = [net.landing("half%d%d" % (h, piece), q_all.at[c, y, h, :, cols], core_peer) for h in range(2)]
 
@@ -336,7 +330,7 @@
         carried[yy] = comb[c, yy] - out
 
     for half, name in ((near, "near"), (far, "far")):
-        for piece in range(2):
+        for piece in range(len(PIECES)):
             for k in (1, 3, 2):
                 take("%s%d_%d" % (name, piece, k))
                 hand_on("core", (y + 4 - k) % 4, half, piece, core_peer)
@@ -398,9 +392,7 @@
             pltpu.VMEM((2, HALF, WIDTH), F32),
             pltpu.VMEM((4, HALF, WIDTH), F32),
             pltpu.VMEM((MATS, RANK, 128), F32),
-            pltpu.VMEM((MATS, RANK, 128), F32),
-            pltpu.VMEM((MATS, RANK, 128), F32),
-            pltpu.VMEM((4, 16, 128), F32),
+            pltpu.VMEM((8, 16, 128), F32),
             pltpu.VMEM((4, 16, 128), F32),
             pltpu.VMEM((8, 16, 128), F32),
             pltpu.VMEM((RANK, 128), F32),

time: 45 us -> 43 us (0.956)
  Pallas kernels: 44.3 us -> 42.2 us
    pallas_call x1, Pallas kernels: 41.8 us -> 39.8 us  [reduce_call(): pl.pallas_call(reduce_kernel, name=name, out_shape=(jax.ShapeDtypeStruct(...]
where the time goes in v4:
time: 43 us; the launch traced here: 42.9 us
  Pallas kernels  42.2 us (98%)
  between operations  0.64 us (1%)
    pallas_call x1, Pallas kernels, reduce_call(): pl.pallas_call(reduce_kernel, name=name, out_shape=(jax.ShapeDtypeStruct(...  39.8 us
    pallas_call x1, Pallas kernels, per_device(): pl.pallas_call(write_kernel, name='write', out_shape=(jax.ShapeDtypeStruc...  2.44 us

profile of v4, /device:TPU:1, one launch (start us, length us, event | category | flops | bytes accessed | tf_op | source)
XLA Modules:
  0.0 42.9 jit_solution(9490257501884501314)
XLA Ops:
  0.6 39.8 %reduce.1 = (f32[2,4,96,896]{3,2,1,0:T(8,128)S(1)}, f32[2,4,2,16,896]{4,3,2,1,0:T(8,128)S(1)}, bf16[2,96,128]{2,1,0:T(8,128)(2,1)S(1)}, f32[4,96,896]{2,1,0:T(8,128)S(1)}, f32[4,96,896]{2,1,0:T(8,128)S(1)}) custom-call(bf16[1,2,96,3584]{3,2,1,0:T(8,128)(2,1)} %g_hbm.1, f32[1,2,96,3584]{3,2,1,0:T(8,128)} %f_hbm.1, f32[2,32,3584]{2,1,0:T(8,128)} %bitcast.1), custom_call_target="tpu_custom_call" | custom-call | tf_op jit(solution)/shard_map/reduce/pallas_call | solution.py:374
  40.4 2.4 %write.1 = (f32[2,96,3584]{2,1,0:T(8,128)}, f32[1,2,96,3584]{3,2,1,0:T(8,128)}) custom-call(f32[2,4,96,896]{3,2,1,0:T(8,128)S(1)} %get-tuple-element.7.comb, f32[2,4,2,16,896]{4,3,2,1,0:T(8,128)S(1)} %get-tuple-element.8.q_all, bf16[2,96,128]{2,1,0:T(8,128)(2,1)S(1)} %get-tuple-element.9.w_ref, f32[4,96,896]{2,1,0:T(8,128)S(1)} %get-tuple-element.10.own_decoded, ...), custom_call_target="tpu_custom_call" | custom-call | tf_op jit(solution)/shard_map/write/pallas_call | solution.py:415

commit v5 on v4

--- a/solution.py
+++ b/solution.py
@@ -10,10 +10,12 @@
 BF16 = jnp.bfloat16
 MATS, ROWS, RANK, COLS = 2, 96, 32, 3584
 WIDTH = 896
-PIECES = ((0, 256), (256, 256), (512, 256), (768, 128))
+PIECES = ((0, 384), (384, 256), (640, 256))
+RING = (pl.ds(0, 640), pl.ds(640, 256))
 HALF = ROWS // 2
 REPLICAS = 32
-TAGS = 56
+BLOCK = 4
+TAGS = 36
 VMEM_BYTES = 32 << 20
 
 
@@ -38,10 +40,12 @@
     col = lax.broadcasted_iota(jnp.int32, (RANK, RANK), 1)
     eye = jnp.where(row == col, 1.0, 0.0).astype(F32)
     inv = eye
-    for k in range(RANK - 1):
-        scale = 1.0 / gram[k : k + 1, k : k + 1]
-        factor = jnp.where(row > k, jnp.broadcast_to(gram[:, k : k + 1], (RANK, RANK)), 0.0)
-        gram, inv = (a - factor * (a[k : k + 1, :] * scale) for a in (gram, inv))
+    for start in range(0, RANK, BLOCK):
+        columns = [jnp.broadcast_to(gram[:, k : k + 1], (RANK, RANK)) for k in range(start, start + BLOCK)]
+        for j, k in enumerate(range(start, start + BLOCK)):
+            factor = jnp.where(row > k, columns[j] * (1.0 / columns[j][k : k + 1, :]), 0.0)
+            gram, inv = (a - factor * a[k : k + 1, :] for a in (gram, inv))
+            columns[j + 1 :] = [a - factor * a[k : k + 1, :] for a in columns[j + 1 :]]
     diag = jnp.sum(gram * eye, axis=1, keepdims=True)
     l_inv = inv * lax.rsqrt(diag)
     orth_t = exact(l_inv, p_t, ((1,), (0,)))
@@ -56,7 +60,7 @@
 class Net:
     def __init__(self, send_sem, recv_sem):
         self.send_sem, self.recv_sem = send_sem, recv_sem
-        self.tags, self.due, self.sent, self.last = {}, {}, [], []
+        self.tags, self.due, self.last = {"": 0}, {}, []
 
     def copy(self, tag, src, dst, to):
         return pltpu.make_async_remote_copy(
@@ -69,8 +73,7 @@
         )
 
     def send(self, tag, src, dst, to):
-        self.sent.append(self.copy(tag, src, dst, to))
-        self.sent[-1].start()
+        self.copy(tag, src, dst, to).start()
 
     def landing(self, tag, ref, to):
         return self.copy(tag, ref, ref, to).wait_recv
@@ -84,11 +87,11 @@
     def at_end(self, step):
         self.last.append(step)
 
-    def finish(self):
+    def finish(self, totals, to):
         for tag in list(self.due):
             self.take(tag)
-        for copy in self.sent:
-            copy.wait_send()
+        for ref in totals:
+            self.copy("", ref, ref, to).wait_send()
         for step in self.last:
             step()
 
@@ -132,6 +135,15 @@
     y_next, y_prev, y_far = (y + 1) % 4, (y + 3) % 4, (y + 2) % 4
     mat = y // 2
 
+    barrier = pltpu.get_barrier_semaphore()
+
+    def greet(peers):
+        for to in peers:
+            pl.semaphore_signal(barrier, inc=1, device_id=to, device_id_type=MESH)
+
+    z_peers = [z_at(k) for k in (4, 3, 5, 2, 6, 1, 7)]
+    greet(z_peers)
+
     pairs = [(1 - c, 1 - mat), (c, 1 - mat), (1 - c, mat), (c, mat)]
     loads = []
     for i, (cc, mm) in enumerate(pairs):
@@ -139,19 +151,18 @@
         loads.append(
             (
                 pltpu.make_async_copy(f_hbm.at[0, mm, :, cols], f_buf.at[i], load_sem.at[i]),
-                pltpu.make_async_copy(g_hbm.at[0, mm, :, cols], g_buf.at[i], load_sem.at[4 + i]),
+                pltpu.make_async_copy(g_hbm.at[0, mm, :, cols], g_buf.at[i], load_sem.at[i]),
             )
         )
-    right_load = pltpu.make_async_copy(r_hbm, r_buf, load_sem.at[8])
+    right_load = pltpu.make_async_copy(r_hbm, r_buf, load_sem.at[4])
     right_load.start()
     for copies in loads:
         for copy in copies:
             copy.start()
 
-    barrier = pltpu.get_barrier_semaphore()
-    peers = [core_peer] + [at(y_=(y + k) % 4, c_=1 - c) for k in (1, 2, 3)] + [f(k) for f, n in ((y_at, 4), (x_at, 4), (z_at, 8)) for k in range(1, n)]
-    for to in peers:
-        pl.semaphore_signal(barrier, inc=1, device_id=to, device_id_type=MESH)
+    near_peers = [core_peer] + [at(y_=(y + k) % 4, c_=cc) for k in (2, 1, 3) for cc in (c, 1 - c)]
+    near_peers += [x_at(k) for k in (2, 1, 3)]
+    greet(near_peers)
     p_own[...] = jnp.zeros(p_own.shape, F32)
     p_sums = {}
 
@@ -190,30 +201,58 @@
     right_load.wait()
     for i in range(4):
         wait_load(i)
-        if i == 0:
-            pl.semaphore_wait(barrier, len(peers))
-        for name, yy in ((("far", y_far), ("across", y_across)), (("beside", y_beside), ("own", y)))[i // 2]:
+        for yy in ((y_far, y_across), (y_beside, y))[i // 2]:
             combine(i, yy)
-            if i % 2 == 0:
-                to_core("c_" + name, yy)
             left_product(i, yy)
         if i % 2 == 1:
             left_sum(i // 2)
+    pl.semaphore_wait(barrier, len(z_peers) + len(near_peers))
+    to_core("c_far", y_far)
 
     ranks = pl.ds(pl.multiple_of(c * 16, 16), 16)
-    for k in (2, 1, 3, 0):
-        for same in ((0, 1) if k else (0,)):
-            cc = c if same else 1 - c
-            part = p_own.at[(y + k) % 4 // 2, pl.ds(pl.multiple_of(cc * 16, 16), 16)]
-            send("p_y", part, p_y.at[2 * y + c], at(y_=(y + k) % 4, c_=cc))
+
+    def to_place(k, cc):
+        part = p_own.at[(y + k) % 4 // 2, pl.ds(pl.multiple_of(cc * 16, 16), 16)]
+        send("p_y", part, p_y.at[2 * y + c], at(y_=(y + k) % 4, c_=cc))
+
+    for k in (2, 1, 3):
+        for cc in (c, 1 - c):
+            to_place(k, cc)
+
+    def ring_first(part):
+        cols = RING[part]
+        send("r_top%d" % part, s_buf.at[y_far, top, cols], r1.at[0, :, cols], y_at(1))
+        send("r_low%d" % part, s_buf.at[y_far, low, cols], r1.at[1, :, cols], y_at(3))
+        net.expect("r_top%d" % part, r1.at[0, :, cols], y_at(1))
+        net.expect("r_low%d" % part, r1.at[1, :, cols], y_at(3))
+
+    def ring_second(part):
+        cols, tag = RING[part], "r_end%d" % part
+        send(tag, s_buf.at[y_next, low, cols], r2.at[0, :, cols], y_at(1))
+        send(tag, s_buf.at[y_prev, top, cols], r2.at[1, :, cols], y_at(3))
+        take("r_top%d" % part)
+        s_buf[y_next, top, cols] += r1[0, :, cols]
+        send(tag, s_buf.at[y_next, top, cols], r2.at[2, :, cols], y_at(1))
+        take("r_low%d" % part)
+        s_buf[y_prev, low, cols] += r1[1, :, cols]
+        send(tag, s_buf.at[y_prev, low, cols], r2.at[3, :, cols], y_at(3))
+        net.expect(tag, r2.at[:, :, cols], core_peer)
+
+    def ring_end(part):
+        cols = RING[part]
+        take("r_end%d" % part)
+        s_buf[y, top, cols] = (s_buf[y, top, cols] + r2[1, :, cols]) + r2[2, :, cols]
+        s_buf[y, low, cols] = (s_buf[y, low, cols] + r2[0, :, cols]) + r2[3, :, cols]
+
+    sum_cores("c_far", y_far)
+    ring_first(0)
+    ring_first(1)
+    to_place(0, 1 - c)
     net.expect("p_y", p_y.at[pl.ds(0, 7)], core_peer)
     p_y[2 * y + c] = p_own[mat, ranks]
-
-    sum_cores("c_far", y_far)
-    send("r_top", s_buf.at[y_far, top], r1.at[0], y_at(1))
-    send("r_low", s_buf.at[y_far, low], r1.at[1], y_at(3))
-    net.expect("r_top", r1.at[0], y_at(1))
-    net.expect("r_low", r1.at[1], y_at(3))
+    to_core("c_across", y_across)
+    to_core("c_beside", y_beside)
+    to_core("c_own", y)
     sum_cores("c_across", y_across)
     sum_cores("c_beside", y_beside)
     sum_cores("c_own", y)
@@ -223,40 +262,31 @@
     for k in (2, 1, 3):
         send("p_x", p_x.at[x], p_x.at[x], x_at(k))
     net.expect("p_x", p_x.at[pl.ds(0, 3)], core_peer)
-    send("r_end", s_buf.at[y_next, low], r2.at[0], y_at(1))
-    send("r_end", s_buf.at[y_prev, top], r2.at[1], y_at(3))
-    net.expect("r_end", r2, core_peer)
-    take("r_top")
-    s_buf[y_next, top] += r1[0]
-    send("r_end", s_buf.at[y_next, top], r2.at[2], y_at(1))
-    take("r_low")
-    s_buf[y_prev, low] += r1[1]
-    send("r_end", s_buf.at[y_prev, low], r2.at[3], y_at(3))
+    ring_second(0)
 
     take("p_x")
     p_z[z] = tree_sum([p_x[i] for i in range(4)])
     for k in (4, 3, 5, 2, 6, 1, 7):
         send("p_z", p_z.at[z], p_z.at[z], z_at(k))
     net.expect("p_z", p_z.at[pl.ds(0, 7)], core_peer)
+    ring_second(1)
     take("p_z")
     p_full[ranks] = tree_sum([p_z[i] for i in range(8)]) * (1.0 / REPLICAS)
     send("p_full", p_full.at[ranks], p_full.at[ranks], core_peer)
     net.expect("p_full", p_full.at[pl.ds(pl.multiple_of(16 - c * 16, 16), 16)], core_peer)
+    ring_end(0)
     take("p_full")
-    take("r_end")
-    s_buf[y, top] = (s_buf[y, top] + r2[1]) + r2[2]
-    s_buf[y, low] = (s_buf[y, low] + r2[0]) + r2[3]
-
-    near = zl // 2
+
+    near = (zl + 2) // 3
     far = 1 - near
-    owner = (zl == 1) | (zl == 2)
+    owner = (zl == 0) | (zl == 2)
 
     def cols_of(piece):
         return pl.ds(*PIECES[piece])
 
     def to_owner(h, piece):
         cols = cols_of(piece)
-        return net.copy("z_sum%d" % piece, q_part.at[h, :, cols], z_part.at[zl, :, cols], at(zl_=1 + h))
+        return net.copy("z_sum%d" % piece, q_part.at[h, :, cols], z_part.at[zl, :, cols], at(zl_=2 * h))
 
     def from_owner(h, k, piece):
         mine = q_all.at[c, y, h, :, cols_of(piece)]
@@ -265,31 +295,37 @@
     left = jnp.concatenate(split(p_full[:, :ROWS]), axis=0)
     for piece in range(len(PIECES)):
         cols = cols_of(piece)
+        if piece == len(PIECES) - 1:
+            ring_end(1)
         hi, lo = split(s_buf[y, :, cols])
         prod = dot(left, hi, ((1,), (0,))) + dot(left, lo, ((1,), (0,)))
         q_part[:, :, cols] = (prod[:RANK] + prod[RANK:]).reshape(2, 16, PIECES[piece][1])
         for h in range(2):
-            pl.when(zl != 1 + h)(to_owner(h, piece).start)
+            pl.when(zl != 2 * h)(to_owner(h, piece).start)
 
     @net.at_end
     def _():
-        for piece in range(len(PIECES)):
-            for h in range(2):
-                pl.when(zl != 1 + h)(to_owner(h, piece).wait_send)
+        def sent(ref):
+            net.copy("", ref, ref, core_peer).wait_send()
+
+        sent(q_part.at[0])
 
         @pl.when(owner)
         def _():
-            for piece in range(len(PIECES)):
-                for k in (1, 2, 3):
-                    from_owner(0, k, piece).wait_send()
+            for _ in range(3):
+                sent(q_part.at[0])
+
+        @pl.when(jnp.logical_not(owner))
+        def _():
+            sent(q_part.at[1])
 
     w_t[mat, :, 0:ROWS] = left_times_inverse(p_full[:, :ROWS]) * (1.0 / REPLICAS)
     send("w", w_t.at[mat], w_t.at[mat], y_at(2))
     net.expect("w", w_t.at[1 - mat], y_at(2))
 
-    def hand_on(tag, yy, half, piece, to):
-        part = q_all.at[c, yy, half, :, cols_of(piece)]
-        send(tag, part, part, to)
+    def to_other_core(yy, half):
+        part = q_all.at[c, yy, half]
+        send("core", part, part, core_peer)
 
     for half, name in ((near, "near"), (far, "far")):
         for piece in range(len(PIECES)):
@@ -317,51 +353,67 @@
                                 from_owner(h, k, piece).start()
 
                 pl.when(jnp.logical_not(owner))(land)
+            part = q_all.at[c, y, half, :, cols]
             for k in (2, 1, 3):
-                tag = "%s%d_%d" % (name, piece, k)
-                hand_on(tag, y, half, piece, y_at(k))
-                net.expect(tag, q_all.at[c, (y + 4 - k) % 4, half, :, cols], core_peer)
-            hand_on("core", y, half, piece, core_peer)
+                send("%s%d" % (name, k), part, part, y_at(k))
+        for k in (1, 2, 3):
+            net.expect("%s%d" % (name, k), q_all.at[c, (y + 4 - k) % 4, half], core_peer)
+        to_other_core(y, half)
     net.expect("core", q_all.at[1 - c], core_peer)
 
     def decode_own(yy):
         out = decode(w_out[yy // 2], q_all[c, yy].reshape(RANK, WIDTH))
-        decoded[yy] = out
-        carried[yy] = comb[c, yy] - out
+        cols = pl.ds(pl.multiple_of(yy % 2 * WIDTH, 128), WIDTH)
+        decoded[yy // 2, :, cols] = out
+        carried[yy // 2, :, cols] = comb[c, yy] - out
 
     for half, name in ((near, "near"), (far, "far")):
-        for piece in range(len(PIECES)):
-            for k in (1, 3, 2):
-                take("%s%d_%d" % (name, piece, k))
-                hand_on("core", (y + 4 - k) % 4, half, piece, core_peer)
+        for k in (1, 3, 2):
+            take("%s%d" % (name, k))
+            to_other_core((y + 4 - k) % 4, half)
         if name == "near":
             take("w")
             for i in range(MATS):
                 hi, lo = split(w_t[i, :, 0:ROWS].T)
                 w_out[i] = jnp.concatenate([hi, lo, hi, lo], axis=1)
-            decode_own(y)
-    for k in (1, 3, 2):
+    for k in (0, 1, 3, 2):
         decode_own((y + 4 - k) % 4)
-    net.finish()
+    net.finish(
+        [
+            c_recv,
+            r1,
+            r2,
+            p_y.at[pl.ds(0, 7)],
+            p_x.at[pl.ds(0, 3)],
+            p_z.at[pl.ds(0, 7)],
+            p_full.at[pl.ds(0, 16)],
+            w_t.at[0],
+            q_all.at[0, pl.ds(0, 3)],
+            q_all.at[0],
+        ],
+        core_peer,
+    )
 
 
 def write_kernel(comb, q_all, w_ref, own_decoded, own_carried, decoded, carried, d_buf, c_buf, sem):
     c = lax.axis_index("dp") % 2
     copies = []
 
-    def write(cc, yy, d_ref, c_ref):
-        cols = pl.ds(pl.multiple_of((2 * cc + yy % 2) * WIDTH, 128), WIDTH)
-        for ref, to in ((d_ref, decoded.at[yy // 2, :, cols]), (c_ref, carried.at[0, yy // 2, :, cols])):
+    def write(cc, mat, d_ref, c_ref):
+        cols = pl.ds(pl.multiple_of(cc * 2 * WIDTH, 128), 2 * WIDTH)
+        for ref, to in ((d_ref, decoded.at[mat, :, cols]), (c_ref, carried.at[0, mat, :, cols])):
             copies.append(pltpu.make_async_copy(ref, to, sem.at[0]))
             copies[-1].start()
 
-    for yy in range(4):
-        write(c, yy, own_decoded.at[yy], own_carried.at[yy])
-    for yy in range(4):
-        out = decode(w_ref[yy // 2], q_all[1 - c, yy].reshape(RANK, WIDTH))
-        d_buf[yy] = out
-        c_buf[yy] = comb[1 - c, yy] - out
-        write(1 - c, yy, d_buf.at[yy], c_buf.at[yy])
+    for mat in range(MATS):
+        write(c, mat, own_decoded.at[mat], own_carried.at[mat])
+    for mat in range(MATS):
+        for i in range(2):
+            cols = pl.ds(i * WIDTH, WIDTH)
+            out = decode(w_ref[mat], q_all[1 - c, 2 * mat + i].reshape(RANK, WIDTH))
+            d_buf[mat, :, cols] = out
+            c_buf[mat, :, cols] = comb[1 - c, 2 * mat + i] - out
+        write(1 - c, mat, d_buf.at[mat], c_buf.at[mat])
     for copy in copies:
         copy.wait()
 
@@ -378,8 +430,8 @@
             jax.ShapeDtypeStruct((2, 4, ROWS, WIDTH), F32),
             jax.ShapeDtypeStruct((2, 4, 2, 16, WIDTH), F32),
             jax.ShapeDtypeStruct((MATS, ROWS, 128), BF16),
-            jax.ShapeDtypeStruct((4, ROWS, WIDTH), F32),
-            jax.ShapeDtypeStruct((4, ROWS, WIDTH), F32),
+            jax.ShapeDtypeStruct((MATS, ROWS, 2 * WIDTH), F32),
+            jax.ShapeDtypeStruct((MATS, ROWS, 2 * WIDTH), F32),
         ),
         in_specs=[hbm] * 3,
         out_specs=(vmem,) * 5,
@@ -399,7 +451,7 @@
             pltpu.VMEM((MATS, RANK, 128), F32),
             pltpu.VMEM((2, 16, WIDTH), F32),
             pltpu.VMEM((4, 16, WIDTH), F32),
-            dma((9,)),
+            dma((5,)),
             dma((1,)),
             dma((TAGS,)),
         ],
@@ -422,8 +474,8 @@
         in_specs=[vmem] * 5,
         out_specs=(hbm, hbm),
         scratch_shapes=[
-            pltpu.VMEM((4, ROWS, WIDTH), F32),
-            pltpu.VMEM((4, ROWS, WIDTH), F32),
+            pltpu.VMEM((MATS, ROWS, 2 * WIDTH), F32),
+            pltpu.VMEM((MATS, ROWS, 2 * WIDTH), F32),
             pltpu.SemaphoreType.DMA((1,)),
         ],
         compiler_params=pltpu.CompilerParams(vmem_limit_bytes=VMEM_BYTES),

time: 43 us -> 40.8 us (0.949)
  Pallas kernels: 42.2 us -> 39.8 us
    pallas_call x1, Pallas kernels: 39.8 us -> 37.4 us  [reduce_call(): pl.pallas_call(reduce_kernel, name=name, out_shape=(jax.ShapeDtypeStruct(...]
where the time goes in v5:
time: 40.8 us; the launch traced here: 40.5 us
  Pallas kernels  39.8 us (98%)
  between operations  0.64 us (2%)
    pallas_call x1, Pallas kernels, reduce_call(): pl.pallas_call(reduce_kernel, name=name, out_shape=(jax.ShapeDtypeStruct(...  37.4 us
    pallas_call x1, Pallas kernels, per_device(): pl.pallas_call(write_kernel, name='write', out_shape=(jax.ShapeDtypeStruc...  2.47 us

profile of v5, /device:TPU:1, one launch (start us, length us, event | category | flops | bytes accessed | tf_op | source)
XLA Modules:
  0.0 40.5 jit_solution(15907420592221268704)
XLA Ops:
  0.6 37.4 %reduce.1 = (f32[2,4,96,896]{3,2,1,0:T(8,128)S(1)}, f32[2,4,2,16,896]{4,3,2,1,0:T(8,128)S(1)}, bf16[2,96,128]{2,1,0:T(8,128)(2,1)S(1)}, f32[2,96,1792]{2,1,0:T(8,128)S(1)}, f32[2,96,1792]{2,1,0:T(8,128)S(1)}) custom-call(bf16[1,2,96,3584]{3,2,1,0:T(8,128)(2,1)} %g_hbm.1, f32[1,2,96,3584]{3,2,1,0:T(8,128)} %f_hbm.1, f32[2,32,3584]{2,1,0:T(8,128)} %bitcast.1), custom_call_target="tpu_custom_call" | custom-call | tf_op jit(solution)/shard_map/reduce/pallas_call | solution.py:426
  38.0 2.5 %write.1 = (f32[2,96,3584]{2,1,0:T(8,128)}, f32[1,2,96,3584]{3,2,1,0:T(8,128)}) custom-call(f32[2,4,96,896]{3,2,1,0:T(8,128)S(1)} %get-tuple-element.7.comb, f32[2,4,2,16,896]{4,3,2,1,0:T(8,128)S(1)} %get-tuple-element.8.q_all, bf16[2,96,128]{2,1,0:T(8,128)(2,1)S(1)} %get-tuple-element.9.w_ref, f32[2,96,1792]{2,1,0:T(8,128)S(1)} %get-tuple-element.10.own_decoded, ...), custom_call_target="tpu_custom_call" | custom-call | tf_op jit(solution)/shard_map/write/pallas_call | solution.py:467

commit v6 on v5

--- a/solution.py
+++ b/solution.py
@@ -15,7 +15,7 @@
 HALF = ROWS // 2
 REPLICAS = 32
 BLOCK = 4
-TAGS = 36
+TAGS = 28
 VMEM_BYTES = 32 << 20
 
 
@@ -207,7 +207,6 @@
         if i % 2 == 1:
             left_sum(i // 2)
     pl.semaphore_wait(barrier, len(z_peers) + len(near_peers))
-    to_core("c_far", y_far)
 
     ranks = pl.ds(pl.multiple_of(c * 16, 16), 16)
 
@@ -218,63 +217,69 @@
     for k in (2, 1, 3):
         for cc in (c, 1 - c):
             to_place(k, cc)
-
-    def ring_first(part):
-        cols = RING[part]
-        send("r_top%d" % part, s_buf.at[y_far, top, cols], r1.at[0, :, cols], y_at(1))
-        send("r_low%d" % part, s_buf.at[y_far, low, cols], r1.at[1, :, cols], y_at(3))
-        net.expect("r_top%d" % part, r1.at[0, :, cols], y_at(1))
-        net.expect("r_low%d" % part, r1.at[1, :, cols], y_at(3))
-
-    def ring_second(part):
-        cols, tag = RING[part], "r_end%d" % part
-        send(tag, s_buf.at[y_next, low, cols], r2.at[0, :, cols], y_at(1))
-        send(tag, s_buf.at[y_prev, top, cols], r2.at[1, :, cols], y_at(3))
-        take("r_top%d" % part)
-        s_buf[y_next, top, cols] += r1[0, :, cols]
-        send(tag, s_buf.at[y_next, top, cols], r2.at[2, :, cols], y_at(1))
-        take("r_low%d" % part)
-        s_buf[y_prev, low, cols] += r1[1, :, cols]
-        send(tag, s_buf.at[y_prev, low, cols], r2.at[3, :, cols], y_at(3))
-        net.expect(tag, r2.at[:, :, cols], core_peer)
-
-    def ring_end(part):
-        cols = RING[part]
-        take("r_end%d" % part)
-        s_buf[y, top, cols] = (s_buf[y, top, cols] + r2[1, :, cols]) + r2[2, :, cols]
-        s_buf[y, low, cols] = (s_buf[y, low, cols] + r2[0, :, cols]) + r2[3, :, cols]
-
-    sum_cores("c_far", y_far)
-    ring_first(0)
-    ring_first(1)
+        if k == 2:
+            to_core("c_far", y_far)
     to_place(0, 1 - c)
     net.expect("p_y", p_y.at[pl.ds(0, 7)], core_peer)
     p_y[2 * y + c] = p_own[mat, ranks]
     to_core("c_across", y_across)
     to_core("c_beside", y_beside)
     to_core("c_own", y)
-    sum_cores("c_across", y_across)
-    sum_cores("c_beside", y_beside)
-    sum_cores("c_own", y)
+
+    def ring_first(part):
+        cols = RING[part]
+        send("r_far%d" % part, s_buf.at[y_far, top, cols], r1.at[0, :, cols], y_at(1))
+        send("r_far%d" % part, s_buf.at[y_far, low, cols], r1.at[1, :, cols], y_at(3))
+        net.expect("r_far%d" % part, r1.at[:, :, cols], core_peer)
+
+    def ring_ready(part):
+        cols, tag = RING[part], "r_end%d" % part
+        send(tag, s_buf.at[y_next, low, cols], r2.at[0, :, cols], y_at(1))
+        send(tag, s_buf.at[y_prev, top, cols], r2.at[1, :, cols], y_at(3))
+
+    def ring_second(part):
+        cols, tag = RING[part], "r_end%d" % part
+        take("r_far%d" % part)
+        s_buf[y_next, top, cols] += r1[0, :, cols]
+        send(tag, s_buf.at[y_next, top, cols], r2.at[2, :, cols], y_at(1))
+        s_buf[y_prev, low, cols] += r1[1, :, cols]
+        send(tag, s_buf.at[y_prev, low, cols], r2.at[3, :, cols], y_at(3))
+        net.expect(tag, r2.at[:, :, cols], core_peer)
+
+    def ring_end(part):
+        cols = RING[part]
+        take("r_end%d" % part)
+        s_buf[y, top, cols] = (s_buf[y, top, cols] + r2[1, :, cols]) + r2[2, :, cols]
+        s_buf[y, low, cols] = (s_buf[y, low, cols] + r2[0, :, cols]) + r2[3, :, cols]
+
+    sum_cores("c_far", y_far)
+    ring_first(0)
+    ring_first(1)
 
     take("p_y")
     p_x[x] = tree_sum([p_y[i] for i in range(8)])
     for k in (2, 1, 3):
         send("p_x", p_x.at[x], p_x.at[x], x_at(k))
     net.expect("p_x", p_x.at[pl.ds(0, 3)], core_peer)
-    ring_second(0)
+    sum_cores("c_across", y_across)
+    sum_cores("c_beside", y_beside)
+    ring_ready(0)
 
     take("p_x")
     p_z[z] = tree_sum([p_x[i] for i in range(4)])
     for k in (4, 3, 5, 2, 6, 1, 7):
         send("p_z", p_z.at[z], p_z.at[z], z_at(k))
     net.expect("p_z", p_z.at[pl.ds(0, 7)], core_peer)
+    ring_second(0)
+    ring_ready(1)
     ring_second(1)
+    sum_cores("c_own", y)
     take("p_z")
     p_full[ranks] = tree_sum([p_z[i] for i in range(8)]) * (1.0 / REPLICAS)
     send("p_full", p_full.at[ranks], p_full.at[ranks], core_peer)
     net.expect("p_full", p_full.at[pl.ds(pl.multiple_of(16 - c * 16, 16), 16)], core_peer)
     ring_end(0)
+    halves = [split(s_buf[y, :, pl.ds(*PIECES[piece])]) for piece in range(len(PIECES) - 1)]
     take("p_full")
 
     near = (zl + 2) // 3
@@ -297,7 +302,8 @@
         cols = cols_of(piece)
         if piece == len(PIECES) - 1:
             ring_end(1)
-        hi, lo = split(s_buf[y, :, cols])
+            halves.append(split(s_buf[y, :, cols]))
+        hi, lo = halves[piece]
         prod = dot(left, hi, ((1,), (0,))) + dot(left, lo, ((1,), (0,)))
         q_part[:, :, cols] = (prod[:RANK] + prod[RANK:]).reshape(2, 16, PIECES[piece][1])
         for h in range(2):
@@ -345,19 +351,28 @@
                     z_part[zl, :, cols] = q_part[near, :, cols]
                     net.landing("z_sum%d" % piece, z_part.at[pl.ds(0, 3), :, cols], core_peer)()
                     q_all[c, y, near, :, cols] = tree_sum([z_part[i, :, cols] for i in range(4)])
-                    for h in range(2):
-
-                        @pl.when(near == h)
-                        def _():
-                            for k in (1, 2, 3):
-                                from_owner(h, k, piece).start()
+
+                @pl.when(zl == 2)
+                def _(piece=piece):
+                    for k in (2, 3, 1):
+                        from_owner(1, k, piece).start()
 
                 pl.when(jnp.logical_not(owner))(land)
             part = q_all.at[c, y, half, :, cols]
             for k in (2, 1, 3):
-                send("%s%d" % (name, k), part, part, y_at(k))
-        for k in (1, 2, 3):
-            net.expect("%s%d" % (name, k), q_all.at[c, (y + 4 - k) % 4, half], core_peer)
+                send("far%d" % k if name == "far" else "near", part, part, y_at(k))
+            if name == "near":
+
+                @pl.when(zl == 0)
+                def _(piece=piece):
+                    for k in (1, 2, 3):
+                        from_owner(0, k, piece).start()
+
+        if name == "near":
+            net.expect("near", q_all.at[c, pl.ds(0, 3), half], core_peer)
+        else:
+            for k in (1, 2, 3):
+                net.expect("far%d" % k, q_all.at[c, (y + 4 - k) % 4, half], core_peer)
         to_other_core(y, half)
     net.expect("core", q_all.at[1 - c], core_peer)
 
@@ -368,8 +383,11 @@
         carried[yy // 2, :, cols] = comb[c, yy] - out
 
     for half, name in ((near, "near"), (far, "far")):
+        if name == "near":
+            take("near")
         for k in (1, 3, 2):
-            take("%s%d" % (name, k))
+            if name == "far":
+                take("far%d" % k)
             to_other_core((y + 4 - k) % 4, half)
         if name == "near":
             take("w")

time: 40.8 us -> 40.5 us (level)
  no operation moved by 1% of the time
where the time goes in v6:
time: 40.5 us; the launch traced here: 40.4 us
  Pallas kernels  39.8 us (98%)
  between operations  0.64 us (2%)
    pallas_call x1, Pallas kernels, reduce_call(): pl.pallas_call(reduce_kernel, name=name, out_shape=(jax.ShapeDtypeStruct(...  37.3 us
    pallas_call x1, Pallas kernels, per_device(): pl.pallas_call(write_kernel, name='write', out_shape=(jax.ShapeDtypeStruc...  2.47 us

profile of v6, /device:TPU:1, one launch (start us, length us, event | category | flops | bytes accessed | tf_op | source)
XLA Modules:
  0.0 40.4 jit_solution(5198101318185863667)
XLA Ops:
  0.6 37.3 %reduce.1 = (f32[2,4,96,896]{3,2,1,0:T(8,128)S(1)}, f32[2,4,2,16,896]{4,3,2,1,0:T(8,128)S(1)}, bf16[2,96,128]{2,1,0:T(8,128)(2,1)S(1)}, f32[2,96,1792]{2,1,0:T(8,128)S(1)}, f32[2,96,1792]{2,1,0:T(8,128)S(1)}) custom-call(bf16[1,2,96,3584]{3,2,1,0:T(8,128)(2,1)} %g_hbm.1, f32[1,2,96,3584]{3,2,1,0:T(8,128)} %f_hbm.1, f32[2,32,3584]{2,1,0:T(8,128)} %bitcast.1), custom_call_target="tpu_custom_call" | custom-call | tf_op jit(solution)/shard_map/reduce/pallas_call | solution.py:444
  38.0 2.5 %write.1 = (f32[2,96,3584]{2,1,0:T(8,128)}, f32[1,2,96,3584]{3,2,1,0:T(8,128)}) custom-call(f32[2,4,96,896]{3,2,1,0:T(8,128)S(1)} %get-tuple-element.7.comb, f32[2,4,2,16,896]{4,3,2,1,0:T(8,128)S(1)} %get-tuple-element.8.q_all, bf16[2,96,128]{2,1,0:T(8,128)(2,1)S(1)} %get-tuple-element.9.w_ref, f32[2,96,1792]{2,1,0:T(8,128)S(1)} %get-tuple-element.10.own_decoded, ...), custom_call_target="tpu_custom_call" | custom-call | tf_op jit(solution)/shard_map/write/pallas_call | solution.py:485

commit v7 on v6

--- a/solution.py
+++ b/solution.py
@@ -198,6 +198,19 @@
         for copy in loads[i]:
             copy.wait()
 
+    ranks = pl.ds(pl.multiple_of(c * 16, 16), 16)
+    k_other, k_same = 3 - 2 * (y % 2), 1 + 2 * (y % 2)
+
+    def to_place(k, cc):
+        part = p_own.at[(y + k) % 4 // 2, pl.ds(pl.multiple_of(cc * 16, 16), 16)]
+        send("p_y", part, p_y.at[2 * y + c], at(y_=(y + k) % 4, c_=cc))
+
+    def other_matrix():
+        pl.semaphore_wait(barrier, len(z_peers) + len(near_peers))
+        for k in (2, k_other):
+            for cc in (c, 1 - c):
+                to_place(k, cc)
+
     right_load.wait()
     for i in range(4):
         wait_load(i)
@@ -206,19 +219,10 @@
             left_product(i, yy)
         if i % 2 == 1:
             left_sum(i // 2)
-    pl.semaphore_wait(barrier, len(z_peers) + len(near_peers))
-
-    ranks = pl.ds(pl.multiple_of(c * 16, 16), 16)
-
-    def to_place(k, cc):
-        part = p_own.at[(y + k) % 4 // 2, pl.ds(pl.multiple_of(cc * 16, 16), 16)]
-        send("p_y", part, p_y.at[2 * y + c], at(y_=(y + k) % 4, c_=cc))
-
-    for k in (2, 1, 3):
-        for cc in (c, 1 - c):
-            to_place(k, cc)
-        if k == 2:
-            to_core("c_far", y_far)
+            pl.when(z >= 4 if i == 1 else z < 4)(other_matrix)
+    to_core("c_far", y_far)
+    for cc in (c, 1 - c):
+        to_place(k_same, cc)
     to_place(0, 1 - c)
     net.expect("p_y", p_y.at[pl.ds(0, 7)], core_peer)
     p_y[2 * y + c] = p_own[mat, ranks]

time: 40.5 us -> 40.5 us (level)
  no operation moved by 1% of the time
where the time goes in v7:
time: 40.5 us; the launch traced here: 40.4 us
  Pallas kernels  39.7 us (98%)
  between operations  0.64 us (2%)
    pallas_call x1, Pallas kernels, reduce_call(): pl.pallas_call(reduce_kernel, name=name, out_shape=(jax.ShapeDtypeStruct(...  37.3 us
    pallas_call x1, Pallas kernels, per_device(): pl.pallas_call(write_kernel, name='write', out_shape=(jax.ShapeDtypeStruc...  2.47 us

profile of v7, /device:TPU:1, one launch (start us, length us, event | category | flops | bytes accessed | tf_op | source)
XLA Modules:
  0.0 40.4 jit_solution(11241279274151431220)
XLA Ops:
  0.6 37.3 %reduce.1 = (f32[2,4,96,896]{3,2,1,0:T(8,128)S(1)}, f32[2,4,2,16,896]{4,3,2,1,0:T(8,128)S(1)}, bf16[2,96,128]{2,1,0:T(8,128)(2,1)S(1)}, f32[2,96,1792]{2,1,0:T(8,128)S(1)}, f32[2,96,1792]{2,1,0:T(8,128)S(1)}) custom-call(bf16[1,2,96,3584]{3,2,1,0:T(8,128)(2,1)} %g_hbm.1, f32[1,2,96,3584]{3,2,1,0:T(8,128)} %f_hbm.1, f32[2,32,3584]{2,1,0:T(8,128)} %bitcast.1), custom_call_target="tpu_custom_call" | custom-call | tf_op jit(solution)/shard_map/reduce/pallas_call | solution.py:448
  37.9 2.5 %write.1 = (f32[2,96,3584]{2,1,0:T(8,128)}, f32[1,2,96,3584]{3,2,1,0:T(8,128)}) custom-call(f32[2,4,96,896]{3,2,1,0:T(8,128)S(1)} %get-tuple-element.7.comb, f32[2,4,2,16,896]{4,3,2,1,0:T(8,128)S(1)} %get-tuple-element.8.q_all, bf16[2,96,128]{2,1,0:T(8,128)(2,1)S(1)} %get-tuple-element.9.w_ref, f32[2,96,1792]{2,1,0:T(8,128)S(1)} %get-tuple-element.10.own_decoded, ...), custom_call_target="tpu_custom_call" | custom-call | tf_op jit(solution)/shard_map/write/pallas_call | solution.py:489

commit v8 on v7

--- a/solution.py
+++ b/solution.py
@@ -15,7 +15,7 @@
 HALF = ROWS // 2
 REPLICAS = 32
 BLOCK = 4
-TAGS = 28
+TAGS = 26
 VMEM_BYTES = 32 << 20
 
 
@@ -173,10 +173,8 @@
 
     def to_core(name, yy):
         send(name, comb.at[1 - c, yy], c_recv.at[yy], core_peer)
-        net.expect(name, c_recv.at[yy], core_peer)
-
-    def sum_cores(name, yy):
-        take(name)
+
+    def sum_cores(yy):
         s_buf[yy] = comb[c, yy] + c_recv[yy]
 
     def left_product(i, yy):
@@ -226,9 +224,9 @@
     to_place(0, 1 - c)
     net.expect("p_y", p_y.at[pl.ds(0, 7)], core_peer)
     p_y[2 * y + c] = p_own[mat, ranks]
-    to_core("c_across", y_across)
-    to_core("c_beside", y_beside)
-    to_core("c_own", y)
+    to_core("c_rest", y_across)
+    to_core("c_rest", y_beside)
+    to_core("c_rest", y)
 
     def ring_first(part):
         cols = RING[part]
@@ -256,7 +254,10 @@
         s_buf[y, top, cols] = (s_buf[y, top, cols] + r2[1, :, cols]) + r2[2, :, cols]
         s_buf[y, low, cols] = (s_buf[y, low, cols] + r2[0, :, cols]) + r2[3, :, cols]
 
-    sum_cores("c_far", y_far)
+    net.expect("c_far", c_recv.at[0], core_peer)
+    net.expect("c_rest", c_recv.at[pl.ds(0, 3)], core_peer)
+    take("c_far")
+    sum_cores(y_far)
     ring_first(0)
     ring_first(1)
 
@@ -265,8 +266,9 @@
     for k in (2, 1, 3):
         send("p_x", p_x.at[x], p_x.at[x], x_at(k))
     net.expect("p_x", p_x.at[pl.ds(0, 3)], core_peer)
-    sum_cores("c_across", y_across)
-    sum_cores("c_beside", y_beside)
+    take("c_rest")
+    sum_cores(y_across)
+    sum_cores(y_beside)
     ring_ready(0)
 
     take("p_x")
@@ -277,7 +279,7 @@
     ring_second(0)
     ring_ready(1)
     ring_second(1)
-    sum_cores("c_own", y)
+    sum_cores(y)
     take("p_z")
     p_full[ranks] = tree_sum([p_z[i] for i in range(8)]) * (1.0 / REPLICAS)
     send("p_full", p_full.at[ranks], p_full.at[ranks], core_peer)

time: 40.5 us -> 40.5 us (level)
  no operation moved by 1% of the time
where the time goes in v8:
time: 40.5 us; the launch traced here: 40.4 us
  Pallas kernels  39.7 us (98%)
  between operations  0.64 us (2%)
    pallas_call x1, Pallas kernels, reduce_call(): pl.pallas_call(reduce_kernel, name=name, out_shape=(jax.ShapeDtypeStruct(...  37.3 us
    pallas_call x1, Pallas kernels, per_device(): pl.pallas_call(write_kernel, name='write', out_shape=(jax.ShapeDtypeStruc...  2.47 us

profile of v8, /device:TPU:1, one launch (start us, length us, event | category | flops | bytes accessed | tf_op | source)
XLA Modules:
  0.0 40.4 jit_solution(3374797847709136197)
XLA Ops:
  0.6 37.3 %reduce.1 = (f32[2,4,96,896]{3,2,1,0:T(8,128)S(1)}, f32[2,4,2,16,896]{4,3,2,1,0:T(8,128)S(1)}, bf16[2,96,128]{2,1,0:T(8,128)(2,1)S(1)}, f32[2,96,1792]{2,1,0:T(8,128)S(1)}, f32[2,96,1792]{2,1,0:T(8,128)S(1)}) custom-call(bf16[1,2,96,3584]{3,2,1,0:T(8,128)(2,1)} %g_hbm.1, f32[1,2,96,3584]{3,2,1,0:T(8,128)} %f_hbm.1, f32[2,32,3584]{2,1,0:T(8,128)} %bitcast.1), custom_call_target="tpu_custom_call" | custom-call | tf_op jit(solution)/shard_map/reduce/pallas_call | solution.py:450
  37.9 2.5 %write.1 = (f32[2,96,3584]{2,1,0:T(8,128)}, f32[1,2,96,3584]{3,2,1,0:T(8,128)}) custom-call(f32[2,4,96,896]{3,2,1,0:T(8,128)S(1)} %get-tuple-element.7.comb, f32[2,4,2,16,896]{4,3,2,1,0:T(8,128)S(1)} %get-tuple-element.8.q_all, bf16[2,96,128]{2,1,0:T(8,128)(2,1)S(1)} %get-tuple-element.9.w_ref, f32[2,96,1792]{2,1,0:T(8,128)S(1)} %get-tuple-element.10.own_decoded, ...), custom_call_target="tpu_custom_call" | custom-call | tf_op jit(solution)/shard_map/write/pallas_call | solution.py:491
